TPU v7x, 128 devices: a whole 4x4x4 slice. The times are simulated.
128 devices in a mesh: chan: 16 (over x_hi, y, core), tm: 8 (over x_lo, z).
Axes of the slice: x: 4 (x_hi: 2, x_lo: 2; x = x_hi * 2 + x_lo), y: 4, z: 4, core: 2. Of those that a mesh axis runs over, the one named last changes fastest.
Arguments:
- record: bfloat16 [128, 4096], P('chan', 'tm'), may hold values from -6 to 6
- tail: bfloat16 [128, 255], P('chan'), may hold values from -6 to 6
- templates: bfloat16 [128, 128, 128], P(None, 'chan'), may hold values from -6 to 6
- shifts: int32 [128, 128], P(None, 'chan'), may hold values from 0 to 127
- mask: int32 [128], P('chan'), may hold values 0 or 1
Outputs:
- stack: float32 [128, 4096], P('chan', 'tm')
All inputs are finite; a program needn't handle non-finite values. No bound on the sum of `mask` on one device may be relied on, other than what follows from the above.
Results may differ from a plain program's by a relative error of at most 0.0029.
Values may be sent and summed in bfloat16 or wider, within the bound.
No kernel may reach another device: no remote copies, remote signals or barrier semaphores. Data moves between devices by JAX's collectives and lax.ppermute only.
A program may use at most 64 MiB of HBM per device.

v0:
```python
import jax
import jax.numpy as jnp
from jax import lax
from jax.sharding import PartitionSpec as P


def passed_along(block, axis, distance):
    devices = range(lax.axis_size(axis))
    route = [(i - distance, i) for i in devices if i - distance in devices]
    return lax.ppermute(block, axis, route)


def in_blocks(array, dim, count):
    dims = array.shape
    tiles = array.reshape(*dims[:dim], count, dims[dim] // count, *dims[dim + 1 :])
    return jnp.moveaxis(tiles, dim, 0)


def sent_and_summed(array, axis, dim):
    tiles = in_blocks(array, dim, lax.axis_size(axis))
    arrived = lax.all_to_all(tiles, axis, split_axis=0, concat_axis=0, tiled=True)
    return arrived.sum(axis=0)


def from_everyone(array, axis):
    copies = jnp.broadcast_to(array, (lax.axis_size(axis), *array.shape))
    return lax.all_to_all(copies, axis, split_axis=0, concat_axis=0, tiled=True)


def over_copies(array, axis):
    everything = from_everyone(array, axis)
    return jnp.sum(everything, axis=0)


def unit_templates(templates):
    values = templates.astype(jnp.float32)
    tap_count = templates.shape[2]
    centered = values - jnp.mean(values, axis=2, keepdims=True)
    norm = jnp.sqrt(tap_count * (jnp.mean(centered * centered, axis=2, keepdims=True) + 1e-06))
    return (centered / norm).astype(jnp.bfloat16)


def window_spread(samples, tap_count):
    values = samples.astype(jnp.float32)
    zero = jnp.zeros((values.shape[0], 1), jnp.float32)
    sums = jnp.concatenate([zero, jnp.cumsum(values, axis=1)], axis=1)
    squares = jnp.concatenate([zero, jnp.cumsum(values * values, axis=1)], axis=1)
    window = sums[:, tap_count:] - sums[:, :-tap_count]
    power = squares[:, tap_count:] - squares[:, :-tap_count]
    return jnp.sqrt(power - window * window / tap_count + tap_count * 1e-06)


def align_lags(normed, shift_rows, out_len):
    shift_range = normed.shape[2] - out_len
    bit_count = max(shift_range - 1, 0).bit_length()
    needed = out_len + (1 << bit_count) - 1
    current = normed
    if needed > current.shape[2]:
        current = jnp.pad(current, ((0, 0), (0, 0), (0, needed - current.shape[2])))
    for position in range(bit_count):
        offset = 1 << position
        kept_len = current.shape[2] - offset
        chosen = (shift_rows >> position & 1)[:, :, None] == 1
        current = jnp.where(chosen, current[:, :, offset:], current[:, :, :kept_len])
    return current[:, :, :out_len]


def channel_terms(ext_rows, unit_rows, shift_rows, mask_rows, out_len):
    tap_count = unit_rows.shape[2]
    chan_count = ext_rows.shape[0]
    templ_count = unit_rows.shape[0]
    filters = jnp.transpose(unit_rows, (1, 0, 2)).reshape(chan_count * templ_count, 1, tap_count)
    grouped = lax.conv_general_dilated(
        ext_rows[None, :, :],
        filters,
        (1,),
        "VALID",
        feature_group_count=chan_count,
        preferred_element_type=jnp.float32,
    )[0]
    lag_count = grouped.shape[1]
    product = jnp.transpose(grouped.reshape(chan_count, templ_count, lag_count), (1, 0, 2))
    spread = window_spread(ext_rows, tap_count)
    normed = product / spread[None, :, :]
    aligned = align_lags(normed, shift_rows, out_len)
    return jnp.sum(aligned * mask_rows[None, :, None], axis=1)


def shards(record, tail, templates, shifts, mask):
    tap_count = templates.shape[2]
    out_len = record.shape[1]
    halo_len = tail.shape[1]
    incoming = passed_along(record[:, :halo_len], "tm", -1)
    at_end = lax.axis_index("tm") == lax.axis_size("tm") - 1
    extended = jnp.concatenate([record, jnp.where(at_end, tail, incoming)], axis=1)
    unit = unit_templates(templates)
    weights = mask.astype(jnp.float32)
    summed = sent_and_summed(channel_terms(extended, unit, shifts, weights, out_len), "chan", 0)
    total = over_copies(jnp.sum(weights), "chan")
    return summed * jnp.sqrt(tap_count / jnp.maximum(total, 1.0))


def solution(mesh):
    in_specs = (P("chan", "tm"), P("chan", None), P(None, "chan", None), P(None, "chan"), P("chan"))
    out_specs = P("chan", "tm")
    return jax.shard_map(shards, mesh=mesh, in_specs=in_specs, out_specs=out_specs, check_vma=False)
```

profile of v0, /device:TPU:2, one launch (start us, length us, event | category | flops | bytes accessed | tf_op | source)
XLA Modules:
  0.0 71.2 jit_solution(11614792713827019993)
XLA Ops:
  0.0 0.7 slice.80
  0.7 5.9 %collective-permute-start = (bf16[8,255]{1,0:T(8,128)(2,1)S(1)}, bf16[8,255]{1,0:T(8,128)(2,1)S(1)}, u32[]{:S(2)}, u32[]{:S(2)}) collective-permute-start(bf16[8,255]{1,0:T(8,128)(2,1)S(1)} %slice.80), channel_id=1, source_target_pairs={{1,0},{2,1},{3,2},{4,3},{5,4},{6,5},{7,6},{9,8},{10,9},{11,10},{12... | collective-permute-start | bytes 12248 | tf_op jit(solution)/shard_map/ppermute | solution.py:10
  6.6 1.3 %convert_reduce_fusion.1 = f32[]{:T(128)} fusion(s32[8]{0:T(128)} %param.9), kind=kLoop, calls=%fused_computation.49 | loop fusion | flops 15 | bytes 36 | tf_op jit(solution)/shard_map/reduce_sum | solution.py:99
  8.0 1.3 %broadcast_in_dim.81 = f32[16,1,1]{2,1,0:T(1,128)} broadcast(f32[]{:T(128)} %convert_reduce_fusion.1), dimensions={} | broadcast | bytes 68 | tf_op jit(solution)/shard_map/broadcast_in_dim | solution.py:26
  9.3 6.4 %all-to-all-start.1 = ((f32[16,1,1]{2,1,0:T(1,128)}), f32[16,1,1]{2,1,0:T(1,128)S(1)}, u32[]{:S(2)}, u32[]{:S(2)}) async-start(f32[16,1,1]{2,1,0:T(1,128)} %broadcast_in_dim.81), calls=%async_computation.1 | async-start | bytes 16384 | tf_op jit(solution)/shard_map/all_to_all | solution.py:27
  15.7 1.2 %convert_reduce_fusion = f32[128,8]{0,1:T(8,128)S(1)} fusion(bf16[128,8,128]{2,1,0:T(8,128)(2,1)} %param.7), kind=kLoop, calls=%fused_computation.16 | loop fusion | flops 261120 | bytes 266240 | tf_op jit(solution)/shard_map/reduce_sum | solution.py:38
  16.9 1.3 %fusion.9 = f32[128,8]{0,1:T(8,128)S(1)} fusion(f32[128,8]{0,1:T(8,128)S(1)} %broadcast_multiply_fusion.1, bf16[128,8,128]{2,1,0:T(8,128)(2,1)} %param.7), kind=kLoop, calls=%fused_computation.19 | loop fusion | flops 523264 | bytes 270336 | tf_op jit(solution)/shard_map/reduce_sum | solution.py:39
  18.2 1.3 %fusion.10 = bf16[128,8,128]{2,0,1:T(8,128)(2,1)S(1)} fusion(f32[128,8]{0,1:T(8,128)S(1)} %multiply_sqrt_fusion, f32[128,8]{0,1:T(8,128)S(1)} %broadcast_multiply_fusion.1, bf16[128,8,128]{2,1,0:T(8,128)(2,1)} %param.7), kind=kLoop, calls=%fused_computation.20 | loop fusion | flops 524288 | bytes 532480 | tf_op jit(solution)/shard_map/convert_element_type | solution.py:40
  19.5 0.7 and_compare_fusion.6
  20.2 0.7 convert_element_type.15
  21.0 0.7 fusion.18
  21.7 0.7 fusion.20
  22.5 1.7 %reduce-window.16 = f32[8,6,128]{2,0,1:T(8,128)S(1)} reduce-window(f32[8,6,128]{2,0,1:T(8,128)S(1)} %pad_bitcast_fusion, f32[]{:T(128)} %constant.40.clone.1), window={size=1x1x128 pad=0_0x0_0x127_0}, to_apply=%region_4.5 | reduce-window | flops 780288 | bytes 49156 | tf_op jit(solution)/shard_map/reduce-window.2
  24.4 0.2 reduce-window.19
  24.6 1.7 %reduce-window.14 = f32[8,6,128]{2,0,1:T(8,128)S(1)} reduce-window(f32[8,6,128]{2,0,1:T(8,128)S(1)} %pad_bitcast_fusion.1, f32[]{:T(128)} %constant.40.clone.1), window={size=1x1x128 pad=0_0x0_0x127_0}, to_apply=%region_2.3 | reduce-window | flops 780288 | bytes 49156 | tf_op jit(solution)/shard_map/reduce-window
  26.5 0.2 reduce-window.15
  27.1 0.9 %copy.51 = bf16[1,8,767]{1,0,2:T(2,128)(2,1)S(1)} copy(bf16[1,8,767]{2,1,0:T(8,128)(2,1)S(1)} %get-tuple-element.8) | data formatting | bytes 24544 | tf_op jit(solution)/shard_map/broadcast_in_dim | solution.py:74
  28.1 21.6 %fusion.3 = f32[1,1024,640]{1,0,2:T(1,128)S(1)} fusion(bf16[1,8,767]{1,0,2:T(2,128)(2,1)S(1)} %copy.51, s32[1024]{0:T(1024)S(1)} %copy-done, bf16[1024,128]{0,1:T(8,128)(2,1)S(1)} %copy.50), kind=kOutput, calls=%fused_computation.12 | convolution fusion | flops 1344274432 | bytes 2899952 | tf_op jit(solution)/shard_map/conv_general_dilated | solution.py:73
  49.7 0.9 %divide_bitcast_fusion = f32[128,8,640]{0,1,2:T(8,128)S(1)} fusion(f32[8,128,640]{1,0,2:T(8,128)S(1)} %bitcast.24, f32[8,640]{0,1:T(8,128)S(1)} %copy.56), kind=kLoop, calls=%fused_computation.2 | loop fusion | flops 655360 | bytes 5263360 | tf_op jit(solution)/shard_map/div | solution.py:84
  50.6 0.2 slice_select_fusion
  50.8 0.2 slice_select_fusion.1
  51.0 0.2 slice_select_fusion.2
  51.2 0.2 slice_select_fusion.3
  51.3 0.2 slice_select_fusion.4
  51.5 0.2 slice_select_fusion.5
  51.7 0.3 fusion.22
  52.0 1.0 %fusion.2 = f32[128,512]{0,1:T(8,128)S(1)} fusion(f32[128,8,513]{0,1,2:T(8,128)S(1)} %get-tuple-element.6, f32[128,8,513]{0,1,2:T(8,128)S(1)} %get-tuple-element.5, f32[8]{0:T(128)S(1)} %convert_element_type.15, pred[128,8]{0,1:T(8,128)(4,1)S(1)} %get-tuple-element.9), kind=kLoop, calls=%fused_computation.11 | loop fusion | flops 1507328 | bytes 4457504 | tf_op jit(solution)/shard_map/reduce_sum | solution.py:86
  53.0 0.8 %copy.57 = f32[128,512]{1,0:T(8,128)} copy(f32[128,512]{0,1:T(8,128)S(1)} %fusion.2) | data formatting | bytes 524288 | tf_op jit(solution)/shard_map/reduce_sum | solution.py:86
  53.8 7.2 %all-to-all-start = ((f32[16,8,512]{2,1,0:T(8,128)}), f32[16,8,512]{2,1,0:T(8,128)S(1)}, u32[]{:S(2)}, u32[]{:S(2)}) async-start(f32[16,8,512]{2,1,0:T(8,128)} %bitcast.11), calls=%async_computation | async-start | bytes 524288 | tf_op jit(solution)/shard_map/all_to_all | solution.py:21
  61.0 0.6 reduce_sum.59
  62.4 8.2 %all-to-all-done = f32[16,8,512]{2,1,0:T(8,128)S(1)} async-done(((f32[16,8,512]{2,1,0:T(8,128)}), f32[16,8,512]{2,1,0:T(8,128)S(1)}, u32[]{:S(2)}, u32[]{:S(2)}) %all-to-all-start) | async-done | bytes 262176 | tf_op jit(solution)/shard_map/all_to_all | solution.py:21
  70.6 0.6 broadcast_multiply_fusion
  (20 shorter events, 1.1 us)
Async XLA Ops:
  0.0 28.1 %copy-start = (s32[1024]{0:T(1024)S(1)}, s32[1024]{0:T(1024)}, u32[]{:S(2)}) copy-start(s32[1024]{0:T(1024)} %constant.16.clone.1) | copy-start | bytes 12292
  0.7 20.3 %collective-permute-start = (bf16[8,255]{1,0:T(8,128)(2,1)S(1)}, bf16[8,255]{1,0:T(8,128)(2,1)S(1)}, u32[]{:S(2)}, u32[]{:S(2)}) collective-permute-start(bf16[8,255]{1,0:T(8,128)(2,1)S(1)} %slice.80), channel_id=1, source_target_pairs={{1,0},{2,1},{3,2},{4,3},{5,4},{6,5},{7,6},{9,8},{10,9},{11,10},{12... | collective-permute-start | bytes 12248 | tf_op jit(solution)/shard_map/ppermute | solution.py:10
  9.3 44.5 %all-to-all-start.1 = ((f32[16,1,1]{2,1,0:T(1,128)}), f32[16,1,1]{2,1,0:T(1,128)S(1)}, u32[]{:S(2)}, u32[]{:S(2)}) async-start(f32[16,1,1]{2,1,0:T(1,128)} %broadcast_in_dim.81), calls=%async_computation.1 | async-start | bytes 16384 | tf_op jit(solution)/shard_map/all_to_all | solution.py:27
  53.8 16.8 %all-to-all-start = ((f32[16,8,512]{2,1,0:T(8,128)}), f32[16,8,512]{2,1,0:T(8,128)S(1)}, u32[]{:S(2)}, u32[]{:S(2)}) async-start(f32[16,8,512]{2,1,0:T(8,128)} %bitcast.11), calls=%async_computation | async-start | bytes 524288 | tf_op jit(solution)/shard_map/all_to_all | solution.py:21
where the time goes:
time: 71.7 us; the launch traced here: 71.2 us
  matrix products  21.6 us (30%)
  starting transfers between devices  19.6 us (27%)
  other arithmetic  15.9 us (22%)
  waiting for transfers between devices  8.21 us (11%)
  local copies, waits for them, and re-layouts  4.94 us (7%)
  between operations  0.94 us (1%)
    conv_general_dilated x1, matrix products, channel_terms(): lax.conv_general_dilated(ext_rows[None, :, :], filters, (1,), 'VALID', fe...  21.6 us
    all_to_all x1, waiting for transfers between devices, sent_and_summed(): lax.all_to_all(tiles, axis, split_axis=0, concat_axis=0, tiled=True)  8.2 us
    all_to_all x1, starting transfers between devices, sent_and_summed(): lax.all_to_all(tiles, axis, split_axis=0, concat_axis=0, tiled=True)  7.22 us
    all_to_all x1, starting transfers between devices, from_everyone(): return lax.all_to_all(copies, axis, split_axis=0, concat_axis=0, tiled=True)  6.43 us
    ppermute x1, starting transfers between devices, passed_along(): return lax.ppermute(block, axis, route)  5.91 us
    another operation x5, other arithmetic  3.81 us
  transfers between devices with their start and end apart: 3, of which 1 were waited for; matrix products, arithmetic and copies ran while one was open for 58% of the time, Pallas kernels for 0%

commit v1 on v0

v1 whole, which is shorter than its diff:
```python
import jax
import jax.numpy as jnp
from jax import lax
from jax.experimental import pallas as pl
from jax.experimental.pallas import tpu as pltpu
from jax.sharding import PartitionSpec as P

LANES = 128
ROWS = 16


def rolled_left(x, distance):
    if distance == 0:
        return x
    return pltpu.roll(x, x.shape[1] - distance, 1)


def window_total(x, tap_count):
    width = 1
    while width < tap_count:
        x = x + rolled_left(x, width)
        width *= 2
    return x


def kernel(axis, rec_ref, nxt_ref, tail_ref, templ_ref, shift_ref, mask_ref, out_ref,
           ext_ref, unit_ref, rolled_ref, prod_ref, index_ref):
    chan_count, out_len = rec_ref.shape
    halo_len = tail_ref.shape[1]
    templ_count = out_ref.shape[0]
    tap_count = templ_ref.shape[1]
    ext_len = ext_ref.shape[1]
    lag_count = prod_ref.shape[2]
    f32 = jnp.float32

    values = templ_ref[...].astype(f32)
    centered = values - jnp.mean(values, axis=1, keepdims=True)
    power = jnp.mean(centered * centered, axis=1, keepdims=True)
    unit_ref[...] = centered * lax.rsqrt(tap_count * (power + 1e-06))

    ext_ref[:, :out_len] = rec_ref[...].astype(f32)
    at_end = lax.axis_index(axis) == lax.axis_size(axis) - 1

    @pl.when(at_end)
    def _():
        ext_ref[:, out_len:] = jnp.zeros((chan_count, ext_len - out_len), f32)
        ext_ref[:, out_len:out_len + halo_len] = tail_ref[...].astype(f32)

    @pl.when(jnp.logical_not(at_end))
    def _():
        ext_ref[:, out_len:] = nxt_ref[:, :ext_len - out_len].astype(f32)

    ext = ext_ref[...]
    weights = jnp.transpose(mask_ref[...]).astype(f32)
    window = window_total(ext, tap_count)
    squares = window_total(ext * ext, tap_count)
    scale = weights * lax.rsqrt(squares - window * window / tap_count + tap_count * 1e-06)
    for i in range(ROWS):
        shifted = rolled_left(ext, i)
        for b in range(ext_len // LANES):
            rolled_ref[b, i * chan_count:(i + 1) * chan_count, :] = shifted[:, b * LANES:(b + 1) * LANES]

    shifts = jnp.transpose(shift_ref[...])
    for c in range(chan_count):
        base = jnp.concatenate(
            [rolled_ref[b, pl.ds(c, ROWS, stride=chan_count), :] for b in range(ext_len // LANES)], axis=1)
        base = base.astype(jnp.bfloat16)
        lagged = jnp.concatenate(
            [rolled_left(base, g * ROWS)[:, :lag_count] for g in range(tap_count // ROWS)], axis=0)
        unit = unit_ref[pl.ds(c, templ_count, stride=chan_count), :].astype(jnp.bfloat16)
        product = jnp.dot(unit, lagged, preferred_element_type=f32)
        prod_ref[c] = product * scale[c:c + 1, :lag_count]
        index_ref[c] = jnp.broadcast_to(shifts[:, c:c + 1], (templ_count, LANES))

    lane = lax.broadcasted_iota(jnp.int32, (8, LANES), 1)
    blocks = out_len // LANES
    for k in range(0, templ_count, 16):
        halves = []
        for r in (k, k + 8):
            rows = slice(r, r + 8)
            totals = [jnp.zeros((8, LANES), f32)] * blocks
            for c in range(chan_count):
                shift = index_ref[c, rows, :]
                place = (lane + shift) & (LANES - 1)
                stays = lane >= shift
                for b in range(blocks):
                    here = prod_ref[c, rows, b * LANES:(b + 1) * LANES]
                    after = prod_ref[c, rows, (b + 1) * LANES:(b + 2) * LANES]
                    mixed = jnp.where(stays, here, after)
                    totals[b] = totals[b] + jnp.take_along_axis(mixed, place, axis=1)
            halves.append(jnp.concatenate(totals, axis=1))
        out_ref[k:k + 16, :out_len] = jnp.concatenate(halves, axis=0).astype(jnp.bfloat16)
    count = jnp.sum(weights, axis=0, keepdims=True)
    out_ref[:, out_len:] = jnp.broadcast_to(count, (templ_count, LANES)).astype(jnp.bfloat16)


def partial_stack(record, nxt, tail, templates, shifts, mask):
    templ_count, chan_count, tap_count = templates.shape
    out_len = record.shape[1]
    ext_len = out_len + 2 * LANES
    lag_count = out_len + LANES
    vmem = pl.BlockSpec(memory_space=pltpu.VMEM)
    return pl.pallas_call(
        lambda *refs: kernel("tm", *refs),
        out_shape=jax.ShapeDtypeStruct((templ_count, out_len + LANES), jnp.bfloat16),
        in_specs=[vmem] * 6,
        out_specs=vmem,
        scratch_shapes=[
            pltpu.VMEM((chan_count, ext_len), jnp.float32),
            pltpu.VMEM((templ_count * chan_count, tap_count), jnp.float32),
            pltpu.VMEM((ext_len // LANES, ROWS * chan_count, LANES), jnp.float32),
            pltpu.VMEM((chan_count, templ_count, lag_count), jnp.float32),
            pltpu.VMEM((chan_count, templ_count, LANES), jnp.int32),
        ],
        compiler_params=pltpu.CompilerParams(vmem_limit_bytes=32 * 1024 * 1024),
        name="partial_stack",
    )(record, nxt, tail, templates.reshape(templ_count * chan_count, tap_count), shifts.T, mask.reshape(1, -1))


def shards(record, tail, templates, shifts, mask):
    tap_count = templates.shape[2]
    out_len = record.shape[1]
    size = lax.axis_size("tm")
    nxt = lax.ppermute(record, "tm", [(i, i - 1) for i in range(1, size)])
    partial = partial_stack(record, nxt, tail, templates, shifts, mask)
    groups = lax.axis_size("chan")
    tiles = partial.reshape(groups, -1, partial.shape[1])
    arrived = lax.all_to_all(tiles, "chan", split_axis=0, concat_axis=0, tiled=True)
    summed = jnp.sum(arrived.astype(jnp.float32), axis=0)
    count = jnp.maximum(summed[:, out_len:out_len + 1], 1.0)
    return summed[:, :out_len] * jnp.sqrt(tap_count / count)


def solution(mesh):
    in_specs = (P("chan", "tm"), P("chan", None), P(None, "chan", None), P(None, "chan"), P("chan"))
    return jax.shard_map(shards, mesh=mesh, in_specs=in_specs, out_specs=P("chan", "tm"), check_vma=False)
```

time: 71.7 us -> 30.1 us (0.42)
  the two profiles are of different devices: /device:TPU:2 before, /device:TPU:96 now
where the time goes in v1:
time: 30.1 us; the launch traced here: 29.8 us
  blocking collectives  15.4 us (51%)
  waiting for transfers between devices  5.55 us (18%)
  local copies, waits for them, and re-layouts  2.99 us (10%)
  Pallas kernels  2.52 us (8%)
  starting transfers between devices  2.43 us (8%)
  other arithmetic  0.84 us (3%)
    all_to_all x1, blocking collectives, shards(): lax.all_to_all(tiles, 'chan', split_axis=0, concat_axis=0, tiled=True)  15.4 us
    ppermute x1, waiting for transfers between devices, shards(): nxt = lax.ppermute(record, 'tm', [(i, i - 1) for i in range(1, size)])  5.55 us
    unnamed x10, local copies, waits for them, and re-layouts  2.99 us
    pallas_call x1, Pallas kernels, partial_stack(): pl.pallas_call(lambda *refs: kernel('tm', *refs), out_shape=jax.ShapeDtyp...  2.52 us
    ppermute x1, starting transfers between devices, shards(): nxt = lax.ppermute(record, 'tm', [(i, i - 1) for i in range(1, size)])  2.43 us
    mul x1, other arithmetic, shards(): return summed[:, :out_len] * jnp.sqrt(tap_count / count)  0.69 us
  transfers between devices with their start and end apart: 1, of which 1 were waited for; matrix products, arithmetic and copies ran while one was open for 0% of the time, Pallas kernels for 0%

profile of v1, /device:TPU:96, one launch (start us, length us, event | category | flops | bytes accessed | tf_op | source)
XLA Modules:
  0.0 29.8 jit_solution(3326919861056221472)
XLA Ops:
  0.0 0.0 copy-start.2
  0.0 2.4 %collective-permute-start = (bf16[8,512]{1,0:T(8,128)(2,1)}, bf16[8,512]{1,0:T(8,128)(2,1)S(1)}, u32[]{:S(2)}, u32[]{:S(2)}) collective-permute-start(bf16[8,512]{1,0:T(8,128)(2,1)} %refs_0_.1), channel_id=1, source_target_pairs={{1,0},{2,1},{3,2},{4,3},{5,4},{6,5},{7,6},{9,8},{10,9},{11,10},{12... | collective-permute-start | bytes 24584 | tf_op jit(solution)/shard_map/ppermute | solution.py:124
  2.4 5.5 %collective-permute-done.refs_1_ = bf16[8,512]{1,0:T(8,128)(2,1)S(1)} collective-permute-done((bf16[8,512]{1,0:T(8,128)(2,1)}, bf16[8,512]{1,0:T(8,128)(2,1)S(1)}, u32[]{:S(2)}, u32[]{:S(2)}) %collective-permute-start) | collective-permute-done | bytes 8224 | tf_op jit(solution)/shard_map/ppermute | solution.py:124
  8.0 0.0 copy-start.4
  8.0 0.0 copy-done.2
  8.0 0.7 %copy-done.4 = s32[8]{0:T(128)S(1)} copy-done((s32[8]{0:T(128)S(1)}, s32[8]{0:T(128)}, u32[]{:S(2)}) %copy-start.4) | copy-done | bytes 56
  8.6 0.0 copy-start
  8.6 0.9 %copy-done = bf16[128,8,128]{2,1,0:T(8,128)(2,1)S(1)} copy-done((bf16[128,8,128]{2,1,0:T(8,128)(2,1)S(1)}, bf16[128,8,128]{2,1,0:T(8,128)(2,1)}, u32[]{:S(2)}) %copy-start) | copy-done | bytes 262168
  9.6 0.0 copy-start.1
  9.6 0.7 %copy-done.1 = bf16[8,512]{1,0:T(8,128)(2,1)S(1)} copy-done((bf16[8,512]{1,0:T(8,128)(2,1)S(1)}, bf16[8,512]{1,0:T(8,128)(2,1)}, u32[]{:S(2)}) %copy-start.1) | copy-done | bytes 8216
  10.3 0.0 copy-start.3
  10.3 0.7 %copy-done.3 = s32[128,8]{0,1:T(8,128)S(1)} copy-done((s32[128,8]{0,1:T(8,128)S(1)}, s32[128,8]{0,1:T(8,128)}, u32[]{:S(2)}) %copy-start.3) | copy-done | bytes 4120
  11.0 2.5 %partial_stack.1 = bf16[128,640]{1,0:T(8,128)(2,1)S(1)} custom-call(bf16[8,512]{1,0:T(8,128)(2,1)S(1)} %copy-done.1, bf16[8,512]{1,0:T(8,128)(2,1)S(1)} %collective-permute-done.refs_1_, bf16[8,255]{1,0:T(8,128)(2,1)S(1)} %copy-done.2, bf16[1024,128]{1,0:T(8,128)(2,1)S(1)} %bitcast.5, s32[8,128]{1,0:T(8,128)S(1)} %bitcast.6, s32[1,8]{1,0:T(1,128)S(1)} %bitcast.7), custom_call_target="tpu_custom_call" | custom-call | tf_op jit(solution)/shard_map/partial_stack/pallas_call | solution.py:103
  13.5 15.4 %all_to_all.5 = bf16[16,8,640]{2,1,0:T(8,128)(2,1)S(1)} all-to-all(bf16[16,8,640]{2,1,0:T(8,128)(2,1)S(1)} %bitcast.4), channel_id=1, replica_groups=mesh['chan'=16,'tm'=8] {'chan'}, dimensions={0} | all-to-all | bytes 327680 | tf_op jit(solution)/shard_map/all_to_all | solution.py:128
  28.9 0.1 fusion.2
  29.1 0.7 %slice_multiply_fusion = f32[8,512]{1,0:T(8,128)} fusion(f32[8,640]{1,0:T(8,128)S(1)} %convert_reduce_fusion, f32[8]{0:T(128)S(1)} %fusion.2), kind=kLoop, calls=%fused_computation.1 | loop fusion | flops 4096 | bytes 32800 | tf_op jit(solution)/shard_map/mul | solution.py:131
  (1 shorter events, 0.0 us)
Async XLA Ops:
  0.0 8.0 %copy-start.2 = (bf16[8,255]{1,0:T(8,128)(2,1)S(1)}, bf16[8,255]{1,0:T(8,128)(2,1)}, u32[]{:S(2)}) copy-start(bf16[8,255]{1,0:T(8,128)(2,1)} %refs_2_.1) | copy-start | bytes 12244
  0.0 8.0 %collective-permute-start = (bf16[8,512]{1,0:T(8,128)(2,1)}, bf16[8,512]{1,0:T(8,128)(2,1)S(1)}, u32[]{:S(2)}, u32[]{:S(2)}) collective-permute-start(bf16[8,512]{1,0:T(8,128)(2,1)} %refs_0_.1), channel_id=1, source_target_pairs={{1,0},{2,1},{3,2},{4,3},{5,4},{6,5},{7,6},{9,8},{10,9},{11,10},{12... | collective-permute-start | bytes 24584 | tf_op jit(solution)/shard_map/ppermute | solution.py:124
  8.0 0.7 %copy-start.4 = (s32[8]{0:T(128)S(1)}, s32[8]{0:T(128)}, u32[]{:S(2)}) copy-start(s32[8]{0:T(128)} %param.9) | copy-start | bytes 100
  8.6 0.9 %copy-start = (bf16[128,8,128]{2,1,0:T(8,128)(2,1)S(1)}, bf16[128,8,128]{2,1,0:T(8,128)(2,1)}, u32[]{:S(2)}) copy-start(bf16[128,8,128]{2,1,0:T(8,128)(2,1)} %param.7) | copy-start | bytes 786436
  9.6 0.7 %copy-start.1 = (bf16[8,512]{1,0:T(8,128)(2,1)S(1)}, bf16[8,512]{1,0:T(8,128)(2,1)}, u32[]{:S(2)}) copy-start(bf16[8,512]{1,0:T(8,128)(2,1)} %refs_0_.1) | copy-start | bytes 24580
  10.3 0.7 %copy-start.3 = (s32[128,8]{0,1:T(8,128)S(1)}, s32[128,8]{0,1:T(8,128)}, u32[]{:S(2)}) copy-start(s32[128,8]{0,1:T(8,128)} %param.8) | copy-start | bytes 12292

commit v2 on v1

v2 whole, which is shorter than its diff:
```python
import jax
import jax.numpy as jnp
from jax import lax
from jax.experimental import pallas as pl
from jax.experimental.pallas import tpu as pltpu
from jax.sharding import PartitionSpec as P

LANES = 128
ROWS = 16
VMEM_BYTES = 32 * 1024 * 1024


def rolled_left(x, distance):
    if distance == 0:
        return x
    return pltpu.roll(x, x.shape[1] - distance, 1)


def window_total(x, tap_count):
    width = 1
    while width < tap_count:
        x = x + rolled_left(x, width)
        width *= 2
    return x


def window_scale(ext, weights, tap_count):
    window = window_total(ext, tap_count)
    power = window_total(ext * ext, tap_count)
    return weights * lax.rsqrt(power - window * window / tap_count + tap_count * 1e-06)


def keep_rolled(ext, rolled_ref):
    chan_count, length = ext.shape
    for i in range(ROWS):
        shifted = rolled_left(ext, i)
        for b in range(length // LANES):
            rolled_ref[b, i * chan_count:(i + 1) * chan_count, :] = shifted[:, b * LANES:(b + 1) * LANES]


def lag_matrix(rolled_ref, channel, chan_count, tap_count, lag_count):
    blocks = [rolled_ref[b, pl.ds(channel, ROWS, stride=chan_count), :] for b in range(rolled_ref.shape[0])]
    base = jnp.concatenate(blocks, axis=1).astype(jnp.bfloat16)
    pieces = [rolled_left(base, g * ROWS)[:, :lag_count] for g in range(tap_count // ROWS)]
    return jnp.concatenate(pieces, axis=0)


def aligned_sum(place, lagged_of, blocks, chan_count):
    lane = lax.broadcasted_iota(jnp.int32, (8, LANES), 1)
    totals = [jnp.zeros((8, LANES), jnp.float32)] * blocks
    for c in range(chan_count):
        shift = place(c)
        source = (lane + shift) & (LANES - 1)
        stays = lane >= shift
        for b in range(blocks):
            mixed = jnp.where(stays, lagged_of(c, b), lagged_of(c, b + 1))
            totals[b] = totals[b] + jnp.take_along_axis(mixed, source, axis=1)
    return jnp.concatenate(totals, axis=1)


def early_kernel(rec_hbm, templ_hbm, shift_hbm, mask_ref, unit_out, shift_out, border_out, first_out,
                 rec_ref, templ_ref, shift_ref, unit_ref, rolled_ref, prod_ref, sems):
    f32 = jnp.float32
    chan_count = rec_ref.shape[0]
    templ_count = first_out.shape[0]
    tap_count = templ_ref.shape[1]
    lag_count = prod_ref.shape[2]
    blocks = first_out.shape[1] // LANES
    copies = [pltpu.make_async_copy(src, dst, sems.at[n]) for n, (src, dst) in enumerate(
        ((templ_hbm, templ_ref), (rec_hbm, rec_ref), (shift_hbm, shift_ref)))]
    for copy in copies:
        copy.start()
    for copy in copies:
        copy.wait()

    values = templ_ref[...].astype(f32)
    centered = values - jnp.mean(values, axis=1, keepdims=True)
    power = jnp.mean(centered * centered, axis=1, keepdims=True)
    unit_ref[...] = centered * lax.rsqrt(tap_count * (power + 1e-06))

    ext = rec_ref[...].astype(f32)
    weights = jnp.transpose(mask_ref[...]).astype(f32)
    scale = window_scale(ext, weights, tap_count)
    keep_rolled(ext, rolled_ref)
    shifts = jnp.transpose(shift_ref[...])
    for c in range(chan_count):
        lagged = lag_matrix(rolled_ref, c, chan_count, tap_count, lag_count)
        unit = unit_ref[pl.ds(c, templ_count, stride=chan_count), :].astype(jnp.bfloat16)
        unit_out[c] = unit
        product = jnp.dot(unit, lagged, preferred_element_type=f32) * scale[c:c + 1, :lag_count]
        prod_ref[c] = product
        border_out[c] = product[:, lag_count - LANES:]
        shift_out[c] = jnp.broadcast_to(shifts[:, c:c + 1], (templ_count, LANES))
    for k in range(0, templ_count, ROWS):
        halves = [aligned_sum(lambda c: shift_out[c, r:r + 8, :],
                              lambda c, b: prod_ref[c, r:r + 8, b * LANES:(b + 1) * LANES],
                              blocks, chan_count) for r in (k, k + 8)]
        first_out[k:k + ROWS, :] = jnp.concatenate(halves, axis=0).astype(jnp.bfloat16)


def late_kernel(axis, rec_ref, nxt_ref, tail_ref, mask_ref, unit_ref, shift_ref, border_ref, first_ref, out_ref,
                ext_ref, rolled_ref, prod_ref):
    f32 = jnp.float32
    chan_count, out_len = rec_ref.shape
    halo_len = tail_ref.shape[1]
    templ_count, first_len = first_ref.shape
    tap_count = unit_ref.shape[2]
    lag_count = prod_ref.shape[2]
    blocks = lag_count // LANES
    ext_ref[:, :LANES] = rec_ref[:, out_len - LANES:].astype(f32)
    at_end = lax.axis_index(axis) == lax.axis_size(axis) - 1

    @pl.when(at_end)
    def _():
        ext_ref[:, LANES:] = jnp.zeros((chan_count, 2 * LANES), f32)
        ext_ref[:, LANES:LANES + halo_len] = tail_ref[...].astype(f32)

    @pl.when(jnp.logical_not(at_end))
    def _():
        ext_ref[:, LANES:] = nxt_ref[:, :2 * LANES].astype(f32)

    ext = ext_ref[...]
    weights = jnp.transpose(mask_ref[...]).astype(f32)
    scale = window_scale(ext, weights, tap_count)
    keep_rolled(ext, rolled_ref)
    for c in range(chan_count):
        lagged = lag_matrix(rolled_ref, c, chan_count, tap_count, lag_count)
        prod_ref[c] = jnp.dot(unit_ref[c], lagged, preferred_element_type=f32) * scale[c:c + 1, :lag_count]
    for k in range(0, templ_count, ROWS):
        def lagged_of(c, b):
            rows = slice(r, r + 8)
            return border_ref[c, rows, :] if b == 0 else prod_ref[c, rows, (b - 1) * LANES:b * LANES]
        halves = []
        for r in (k, k + 8):
            halves.append(aligned_sum(lambda c: shift_ref[c, r:r + 8, :], lagged_of, blocks, chan_count))
        out_ref[k:k + ROWS, first_len:out_len] = jnp.concatenate(halves, axis=0).astype(jnp.bfloat16)
    out_ref[:, :first_len] = first_ref[...]
    count = jnp.sum(weights, axis=0, keepdims=True)
    out_ref[:, out_len:] = jnp.broadcast_to(count, (templ_count, LANES)).astype(jnp.bfloat16)


def shards(record, tail, templates, shifts, mask):
    templ_count, chan_count, tap_count = templates.shape
    out_len = record.shape[1]
    early_len = out_len - LANES
    first_len = early_len - LANES
    f32, bf16 = jnp.float32, jnp.bfloat16
    vmem = pl.BlockSpec(memory_space=pltpu.VMEM)
    hbm = pl.BlockSpec(memory_space=pl.ANY)
    params = pltpu.CompilerParams(vmem_limit_bytes=VMEM_BYTES)
    size = lax.axis_size("tm")
    mask_row = mask.reshape(1, chan_count)
    nxt = lax.ppermute(record, "tm", [(i, i - 1) for i in range(1, size)])
    unit, moved, border, first = pl.pallas_call(
        early_kernel,
        out_shape=(
            jax.ShapeDtypeStruct((chan_count, templ_count, tap_count), bf16),
            jax.ShapeDtypeStruct((chan_count, templ_count, LANES), jnp.int32),
            jax.ShapeDtypeStruct((chan_count, templ_count, LANES), f32),
            jax.ShapeDtypeStruct((templ_count, first_len), bf16),
        ),
        in_specs=[hbm] * 3 + [vmem],
        out_specs=(vmem,) * 4,
        scratch_shapes=[
            pltpu.VMEM((chan_count, out_len), bf16),
            pltpu.VMEM((templ_count * chan_count, tap_count), bf16),
            pltpu.VMEM((chan_count, templ_count), jnp.int32),
            pltpu.VMEM((templ_count * chan_count, tap_count), f32),
            pltpu.VMEM((out_len // LANES, ROWS * chan_count, LANES), f32),
            pltpu.VMEM((chan_count, templ_count, early_len), f32),
            pltpu.SemaphoreType.DMA((3,)),
        ],
        compiler_params=params,
        cost_estimate=pl.CostEstimate(flops=200_000_000, bytes_accessed=2_000_000, transcendentals=0),
        name="early_lags",
    )(record, templates.reshape(templ_count * chan_count, tap_count), shifts.T, mask_row)
    partial = pl.pallas_call(
        lambda *refs: late_kernel("tm", *refs),
        out_shape=jax.ShapeDtypeStruct((templ_count, out_len + LANES), bf16),
        in_specs=[vmem] * 8,
        out_specs=vmem,
        scratch_shapes=[
            pltpu.VMEM((chan_count, 3 * LANES), f32),
            pltpu.VMEM((3, ROWS * chan_count, LANES), f32),
            pltpu.VMEM((chan_count, templ_count, 2 * LANES), f32),
        ],
        compiler_params=params,
        name="late_lags",
    )(record, nxt, tail, mask_row, unit, moved, border, first)
    tiles = partial.reshape(lax.axis_size("chan"), -1, partial.shape[1])
    arrived = lax.all_to_all(tiles, "chan", split_axis=0, concat_axis=0, tiled=True)
    summed = jnp.sum(arrived.astype(f32), axis=0)
    count = jnp.maximum(summed[:, out_len:out_len + 1], 1.0)
    return summed[:, :out_len] * jnp.sqrt(tap_count / count)


def solution(mesh):
    in_specs = (P("chan", "tm"), P("chan", None), P(None, "chan", None), P(None, "chan"), P("chan"))
    return jax.shard_map(shards, mesh=mesh, in_specs=in_specs, out_specs=P("chan", "tm"), check_vma=False)
```

time: 30.1 us -> 28.8 us (0.957)
  the two profiles are of different devices: /device:TPU:96 before, /device:TPU:2 now
where the time goes in v2:
time: 28.8 us; the launch traced here: 28.5 us
  blocking collectives  14.8 us (51%)
  starting transfers between devices  6.04 us (21%)
  Pallas kernels  3.81 us (13%)
  local copies, waits for them, and re-layouts  2.96 us (10%)
  other arithmetic  0.84 us (3%)
    all_to_all x1, blocking collectives, shards(): lax.all_to_all(tiles, 'chan', split_axis=0, concat_axis=0, tiled=True)  14.8 us
    ppermute x1, starting transfers between devices, shards(): nxt = lax.ppermute(record, 'tm', [(i, i - 1) for i in range(1, size)])  6.04 us
    unnamed x10, local copies, waits for them, and re-layouts  2.96 us
    pallas_call x1, Pallas kernels, shards(): pl.pallas_call(early_kernel, out_shape=(jax.ShapeDtypeStruct((chan_count,...  2.47 us
    pallas_call x1, Pallas kernels, shards(): pl.pallas_call(lambda *refs: late_kernel('tm', *refs), out_shape=jax.Shap...  1.34 us
    mul x1, other arithmetic, shards(): return summed[:, :out_len] * jnp.sqrt(tap_count / count)  0.69 us
  transfers between devices with their start and end apart: 1, of which 0 were waited for; matrix products, arithmetic and copies ran while one was open for 0% of the time, Pallas kernels for 9%

profile of v2, /device:TPU:2, one launch (start us, length us, event | category | flops | bytes accessed | tf_op | source)
XLA Modules:
  0.0 28.5 jit_solution(16001828449159067668)
XLA Ops:
  0.0 0.0 copy-start.4
  0.0 6.0 %collective-permute-start = (bf16[8,512]{1,0:T(8,128)(2,1)}, bf16[8,512]{1,0:T(8,128)(2,1)S(1)}, u32[]{:S(2)}, u32[]{:S(2)}) collective-permute-start(bf16[8,512]{1,0:T(8,128)(2,1)} %refs_0_.1), channel_id=1, source_target_pairs={{1,0},{2,1},{3,2},{4,3},{5,4},{6,5},{7,6},{9,8},{10,9},{11,10},{12... | collective-permute-start | bytes 24584 | tf_op jit(solution)/shard_map/ppermute | solution.py:153
  6.0 0.0 copy-start.2
  6.1 0.0 copy-done.4
  6.1 0.6 %copy-done.2 = s32[8]{0:T(128)S(1)} copy-done((s32[8]{0:T(128)S(1)}, s32[8]{0:T(128)}, u32[]{:S(2)}) %copy-start.2) | copy-done | bytes 56
  6.7 0.0 copy-start
  6.7 0.7 %copy-done = bf16[8,512]{1,0:T(8,128)(2,1)S(1)} copy-done((bf16[8,512]{1,0:T(8,128)(2,1)S(1)}, bf16[8,512]{1,0:T(8,128)(2,1)}, u32[]{:S(2)}) %copy-start) | copy-done | bytes 8216
  7.4 0.0 copy-start.3
  7.4 0.9 %copy-done.3 = bf16[128,8,128]{2,1,0:T(8,128)(2,1)S(1)} copy-done((bf16[128,8,128]{2,1,0:T(8,128)(2,1)S(1)}, bf16[128,8,128]{2,1,0:T(8,128)(2,1)}, u32[]{:S(2)}) %copy-start.3) | copy-done | bytes 262168
  8.4 2.5 %early_lags.1 = (bf16[8,128,128]{2,1,0:T(8,128)(2,1)S(1)}, s32[8,128,128]{2,1,0:T(8,128)S(1)}, f32[8,128,128]{2,1,0:T(8,128)S(1)}, bf16[128,256]{1,0:T(8,128)(2,1)S(1)}) custom-call(bf16[8,512]{1,0:T(8,128)(2,1)S(1)} %copy-done, bf16[1024,128]{1,0:T(8,128)(2,1)S(1)} %bitcast.7, s32[8,128]{1,0:T(8,128)S(1)} %bitcast.8, s32[1,8]{1,0:T(1,128)S(1)} %bitcast.5), custom_call_target="tpu_custom_call" | custom-call | flops 200000000 | bytes 2000000 | tf_op jit(solution)/shard_map/early_lags/pallas_call | solution.py:154
  10.8 0.0 copy-start.1
  10.8 0.0 collective-permute-done.refs_1_
  10.8 0.7 %copy-done.1 = bf16[8,255]{1,0:T(8,128)(2,1)S(1)} copy-done((bf16[8,255]{1,0:T(8,128)(2,1)S(1)}, bf16[8,255]{1,0:T(8,128)(2,1)}, u32[]{:S(2)}) %copy-start.1) | copy-done | bytes 4104
  11.5 1.3 %late_lags.1 = bf16[128,640]{1,0:T(8,128)(2,1)S(1)} custom-call(bf16[8,512]{1,0:T(8,128)(2,1)S(1)} %copy-done, bf16[8,512]{1,0:T(8,128)(2,1)S(1)} %collective-permute-done.refs_1_, bf16[8,255]{1,0:T(8,128)(2,1)S(1)} %copy-done.1, s32[1,8]{1,0:T(1,128)S(1)} %bitcast.6, bf16[8,128,128]{2,1,0:T(8,128)(2,1)S(1)} %get-tuple-element.9.refs_4_, ...), custom_call_target="tpu_custom_call" | custom-call | tf_op jit(solution)/shard_map/late_lags/pallas_call | solution.py:177
  12.9 14.8 %all_to_all.5 = bf16[16,8,640]{2,1,0:T(8,128)(2,1)S(1)} all-to-all(bf16[16,8,640]{2,1,0:T(8,128)(2,1)S(1)} %bitcast.4), channel_id=1, replica_groups=mesh['chan'=16,'tm'=8] {'chan'}, dimensions={0} | all-to-all | bytes 327680 | tf_op jit(solution)/shard_map/all_to_all | solution.py:191
  27.7 0.1 fusion.2
  27.8 0.7 %slice_multiply_fusion = f32[8,512]{1,0:T(8,128)} fusion(f32[8,640]{1,0:T(8,128)S(1)} %convert_reduce_fusion, f32[8]{0:T(128)S(1)} %fusion.2), kind=kLoop, calls=%fused_computation.1 | loop fusion | flops 4096 | bytes 32800 | tf_op jit(solution)/shard_map/mul | solution.py:194
  (1 shorter events, 0.0 us)
Async XLA Ops:
  0.0 6.1 %copy-start.4 = (s32[128,8]{0,1:T(8,128)S(1)}, s32[128,8]{0,1:T(8,128)}, u32[]{:S(2)}) copy-start(s32[128,8]{0,1:T(8,128)} %param.8) | copy-start | bytes 12292
  0.0 10.8 %collective-permute-start = (bf16[8,512]{1,0:T(8,128)(2,1)}, bf16[8,512]{1,0:T(8,128)(2,1)S(1)}, u32[]{:S(2)}, u32[]{:S(2)}) collective-permute-start(bf16[8,512]{1,0:T(8,128)(2,1)} %refs_0_.1), channel_id=1, source_target_pairs={{1,0},{2,1},{3,2},{4,3},{5,4},{6,5},{7,6},{9,8},{10,9},{11,10},{12... | collective-permute-start | bytes 24584 | tf_op jit(solution)/shard_map/ppermute | solution.py:153
  6.0 0.7 %copy-start.2 = (s32[8]{0:T(128)S(1)}, s32[8]{0:T(128)}, u32[]{:S(2)}) copy-start(s32[8]{0:T(128)} %param.9) | copy-start | bytes 100
  6.7 0.7 %copy-start = (bf16[8,512]{1,0:T(8,128)(2,1)S(1)}, bf16[8,512]{1,0:T(8,128)(2,1)}, u32[]{:S(2)}) copy-start(bf16[8,512]{1,0:T(8,128)(2,1)} %refs_0_.1) | copy-start | bytes 24580
  7.4 0.9 %copy-start.3 = (bf16[128,8,128]{2,1,0:T(8,128)(2,1)S(1)}, bf16[128,8,128]{2,1,0:T(8,128)(2,1)}, u32[]{:S(2)}) copy-start(bf16[128,8,128]{2,1,0:T(8,128)(2,1)} %param.7) | copy-start | bytes 786436
  10.8 0.7 %copy-start.1 = (bf16[8,255]{1,0:T(8,128)(2,1)S(1)}, bf16[8,255]{1,0:T(8,128)(2,1)}, u32[]{:S(2)}) copy-start(bf16[8,255]{1,0:T(8,128)(2,1)} %refs_2_.1) | copy-start | bytes 12244

commit v3 on v2

--- a/solution.py
+++ b/solution.py
@@ -58,8 +58,9 @@
     return jnp.concatenate(totals, axis=1)
 
 
-def early_kernel(rec_hbm, templ_hbm, shift_hbm, mask_ref, unit_out, shift_out, border_out, first_out,
-                 rec_ref, templ_ref, shift_ref, unit_ref, rolled_ref, prod_ref, sems):
+def early_kernel(rec_hbm, tail_hbm, templ_hbm, shift_hbm, mask_hbm,
+                 unit_out, shift_out, border_out, first_out, edge_out, weight_out,
+                 rec_ref, tail_ref, templ_ref, shift_ref, mask_ref, unit_ref, rolled_ref, prod_ref, sems):
     f32 = jnp.float32
     chan_count = rec_ref.shape[0]
     templ_count = first_out.shape[0]
@@ -67,7 +68,7 @@
     lag_count = prod_ref.shape[2]
     blocks = first_out.shape[1] // LANES
     copies = [pltpu.make_async_copy(src, dst, sems.at[n]) for n, (src, dst) in enumerate(
-        ((templ_hbm, templ_ref), (rec_hbm, rec_ref), (shift_hbm, shift_ref)))]
+        ((templ_hbm, templ_ref), (rec_hbm, rec_ref), (shift_hbm, shift_ref), (mask_hbm, mask_ref), (tail_hbm, tail_ref)))]
     for copy in copies:
         copy.start()
     for copy in copies:
@@ -80,6 +81,11 @@
 
     ext = rec_ref[...].astype(f32)
     weights = jnp.transpose(mask_ref[...]).astype(f32)
+    weight_out[...] = jnp.broadcast_to(weights, (chan_count, LANES))
+    halo_len = tail_ref.shape[1]
+    edge_out[...] = jnp.zeros(edge_out.shape, f32)
+    edge_out[:, :LANES] = ext[:, ext.shape[1] - LANES:]
+    edge_out[:, LANES:LANES + halo_len] = tail_ref[...].astype(f32)
     scale = window_scale(ext, weights, tap_count)
     keep_rolled(ext, rolled_ref)
     shifts = jnp.transpose(shift_ref[...])
@@ -98,30 +104,25 @@
         first_out[k:k + ROWS, :] = jnp.concatenate(halves, axis=0).astype(jnp.bfloat16)
 
 
-def late_kernel(axis, rec_ref, nxt_ref, tail_ref, mask_ref, unit_ref, shift_ref, border_ref, first_ref, out_ref,
+def late_kernel(axis, nxt_ref, edge_ref, weight_ref, unit_ref, shift_ref, border_ref, first_ref, out_ref,
                 ext_ref, rolled_ref, prod_ref):
     f32 = jnp.float32
-    chan_count, out_len = rec_ref.shape
-    halo_len = tail_ref.shape[1]
+    chan_count = nxt_ref.shape[0]
     templ_count, first_len = first_ref.shape
     tap_count = unit_ref.shape[2]
     lag_count = prod_ref.shape[2]
     blocks = lag_count // LANES
-    ext_ref[:, :LANES] = rec_ref[:, out_len - LANES:].astype(f32)
+    out_len = first_len + lag_count
     at_end = lax.axis_index(axis) == lax.axis_size(axis) - 1
-
-    @pl.when(at_end)
-    def _():
-        ext_ref[:, LANES:] = jnp.zeros((chan_count, 2 * LANES), f32)
-        ext_ref[:, LANES:LANES + halo_len] = tail_ref[...].astype(f32)
+    ext_ref[...] = edge_ref[...]
 
     @pl.when(jnp.logical_not(at_end))
     def _():
         ext_ref[:, LANES:] = nxt_ref[:, :2 * LANES].astype(f32)
 
     ext = ext_ref[...]
-    weights = jnp.transpose(mask_ref[...]).astype(f32)
-    scale = window_scale(ext, weights, tap_count)
+    weights = weight_ref[...]
+    scale = window_scale(ext, weights[:, :1], tap_count)
     keep_rolled(ext, rolled_ref)
     for c in range(chan_count):
         lagged = lag_matrix(rolled_ref, c, chan_count, tap_count, lag_count)
@@ -146,38 +147,43 @@
     first_len = early_len - LANES
     f32, bf16 = jnp.float32, jnp.bfloat16
     vmem = pl.BlockSpec(memory_space=pltpu.VMEM)
-    hbm = pl.BlockSpec(memory_space=pl.ANY)
+    hbm = pl.BlockSpec(memory_space=pltpu.HBM)
     params = pltpu.CompilerParams(vmem_limit_bytes=VMEM_BYTES)
     size = lax.axis_size("tm")
     mask_row = mask.reshape(1, chan_count)
     nxt = lax.ppermute(record, "tm", [(i, i - 1) for i in range(1, size)])
-    unit, moved, border, first = pl.pallas_call(
+    unit, moved, border, first, edge, weights = pl.pallas_call(
         early_kernel,
         out_shape=(
             jax.ShapeDtypeStruct((chan_count, templ_count, tap_count), bf16),
             jax.ShapeDtypeStruct((chan_count, templ_count, LANES), jnp.int32),
             jax.ShapeDtypeStruct((chan_count, templ_count, LANES), f32),
             jax.ShapeDtypeStruct((templ_count, first_len), bf16),
+            jax.ShapeDtypeStruct((chan_count, 3 * LANES), f32),
+            jax.ShapeDtypeStruct((chan_count, LANES), f32),
         ),
-        in_specs=[hbm] * 3 + [vmem],
-        out_specs=(vmem,) * 4,
+        in_specs=[hbm] * 5,
+        out_specs=(vmem,) * 6,
         scratch_shapes=[
             pltpu.VMEM((chan_count, out_len), bf16),
+            pltpu.VMEM(tail.shape, bf16),
             pltpu.VMEM((templ_count * chan_count, tap_count), bf16),
             pltpu.VMEM((chan_count, templ_count), jnp.int32),
+            pltpu.VMEM((1, chan_count), jnp.int32),
             pltpu.VMEM((templ_count * chan_count, tap_count), f32),
             pltpu.VMEM((out_len // LANES, ROWS * chan_count, LANES), f32),
             pltpu.VMEM((chan_count, templ_count, early_len), f32),
-            pltpu.SemaphoreType.DMA((3,)),
+            pltpu.SemaphoreType.DMA((5,)),
         ],
         compiler_params=params,
         cost_estimate=pl.CostEstimate(flops=200_000_000, bytes_accessed=2_000_000, transcendentals=0),
         name="early_lags",
-    )(record, templates.reshape(templ_count * chan_count, tap_count), shifts.T, mask_row)
+    )(*[pltpu.with_memory_space_constraint(x, pltpu.HBM) for x in (
+        record, tail, templates.reshape(templ_count * chan_count, tap_count), shifts.T, mask_row)])
     partial = pl.pallas_call(
         lambda *refs: late_kernel("tm", *refs),
         out_shape=jax.ShapeDtypeStruct((templ_count, out_len + LANES), bf16),
-        in_specs=[vmem] * 8,
+        in_specs=[vmem] * 7,
         out_specs=vmem,
         scratch_shapes=[
             pltpu.VMEM((chan_count, 3 * LANES), f32),
@@ -186,7 +192,7 @@
         ],
         compiler_params=params,
         name="late_lags",
-    )(record, nxt, tail, mask_row, unit, moved, border, first)
+    )(nxt, edge, weights, unit, moved, border, first)
     tiles = partial.reshape(lax.axis_size("chan"), -1, partial.shape[1])
     arrived = lax.all_to_all(tiles, "chan", split_axis=0, concat_axis=0, tiled=True)
     summed = jnp.sum(arrived.astype(f32), axis=0)

time: 28.8 us -> 26.5 us (0.920)
  local copies, waits for them, and re-layouts: 2.96 us -> 0 us
  Pallas kernels: 3.81 us -> 4.72 us
    unnamed x10 -> x0, local copies, waits for them, and re-layouts: 2.96 us -> none
    pallas_call x1, Pallas kernels: 2.47 us -> 3.41 us  [shards(): pl.pallas_call(early_kernel, out_shape=(jax.ShapeDtypeStruct((chan_count,...]
  transfers between devices with their start and end apart: 1 -> 1, of which waited for: 0 -> 0; matrix products, arithmetic and copies ran while one was open for 0% -> 0% of each run, Pallas kernels for 9% -> 13%
where the time goes in v3:
time: 26.5 us; the launch traced here: 26.3 us
  blocking collectives  14.8 us (56%)
  starting transfers between devices  5.9 us (22%)
  Pallas kernels  4.72 us (18%)
  other arithmetic  0.84 us (3%)
    all_to_all x1, blocking collectives, shards(): lax.all_to_all(tiles, 'chan', split_axis=0, concat_axis=0, tiled=True)  14.8 us
    ppermute x1, starting transfers between devices, shards(): nxt = lax.ppermute(record, 'tm', [(i, i - 1) for i in range(1, size)])  5.9 us
    pallas_call x1, Pallas kernels, shards(): pl.pallas_call(early_kernel, out_shape=(jax.ShapeDtypeStruct((chan_count,...  3.41 us
    pallas_call x1, Pallas kernels, shards(): pl.pallas_call(lambda *refs: late_kernel('tm', *refs), out_shape=jax.Shap...  1.31 us
    mul x1, other arithmetic, shards(): return summed[:, :out_len] * jnp.sqrt(tap_count / count)  0.69 us
  transfers between devices with their start and end apart: 1, of which 0 were waited for; matrix products, arithmetic and copies ran while one was open for 0% of the time, Pallas kernels for 13%

profile of v3, /device:TPU:2, one launch (start us, length us, event | category | flops | bytes accessed | tf_op | source)
XLA Modules:
  0.0 26.3 jit_solution(16061067337217107516)
XLA Ops:
  0.0 5.9 %collective-permute-start = (bf16[8,512]{1,0:T(8,128)(2,1)}, bf16[8,512]{1,0:T(8,128)(2,1)S(1)}, u32[]{:S(2)}, u32[]{:S(2)}) collective-permute-start(bf16[8,512]{1,0:T(8,128)(2,1)} %rec_hbm.1), channel_id=1, source_target_pairs={{1,0},{2,1},{3,2},{4,3},{5,4},{6,5},{7,6},{9,8},{10,9},{11,10},{12... | collective-permute-start | bytes 24584 | tf_op jit(solution)/shard_map/ppermute | solution.py:154
  5.9 3.4 %early_lags.1 = (bf16[8,128,128]{2,1,0:T(8,128)(2,1)S(1)}, s32[8,128,128]{2,1,0:T(8,128)S(1)}, f32[8,128,128]{2,1,0:T(8,128)S(1)}, bf16[128,256]{1,0:T(8,128)(2,...) custom-call(bf16[8,512]{1,0:T(8,128)(2,1)} %rec_hbm.1, bf16[8,255]{1,0:T(8,128)(2,1)} %tail_hbm.1, ...), custom_call_target="tpu_custom_call" | custom-call | flops 200000000 | bytes 2000000 | tf_op jit(solution)/shard_map/early_lags/pallas_call | solution.py:155
  9.3 0.0 collective-permute-done.refs_0_
  9.3 1.3 %late_lags.1 = bf16[128,640]{1,0:T(8,128)(2,1)S(1)} custom-call(bf16[8,512]{1,0:T(8,128)(2,1)S(1)} %collective-permute-done.refs_0_, f32[8,384]{1,0:T(8,128)S(1)} %get-tuple-element.11.refs_1_, f32[8,128]{1,0:T(8,128)S(1)} %get-tuple-element.12.refs_2_, bf16[8,128,128]{2,1,0:T(8,128)(2,1)S(1)} %get-tuple-element.13.refs_3_, ...), custom_call_target="tpu_custom_call" | custom-call | tf_op jit(solution)/shard_map/late_lags/pallas_call | solution.py:183
  10.7 14.8 %all_to_all.5 = bf16[16,8,640]{2,1,0:T(8,128)(2,1)S(1)} all-to-all(bf16[16,8,640]{2,1,0:T(8,128)(2,1)S(1)} %bitcast.4), channel_id=1, replica_groups=mesh['chan'=16,'tm'=8] {'chan'}, dimensions={0} | all-to-all | bytes 327680 | tf_op jit(solution)/shard_map/all_to_all | solution.py:197
  25.5 0.1 fusion.2
  25.6 0.7 %slice_multiply_fusion = f32[8,512]{1,0:T(8,128)} fusion(f32[8,640]{1,0:T(8,128)S(1)} %convert_reduce_fusion, f32[8]{0:T(128)S(1)} %fusion.2), kind=kLoop, calls=%fused_computation.1 | loop fusion | flops 4096 | bytes 32800 | tf_op jit(solution)/shard_map/mul | solution.py:200
  (1 shorter events, 0.0 us)
Async XLA Ops:
  0.0 9.3 %collective-permute-start = (bf16[8,512]{1,0:T(8,128)(2,1)}, bf16[8,512]{1,0:T(8,128)(2,1)S(1)}, u32[]{:S(2)}, u32[]{:S(2)}) collective-permute-start(bf16[8,512]{1,0:T(8,128)(2,1)} %rec_hbm.1), channel_id=1, source_target_pairs={{1,0},{2,1},{3,2},{4,3},{5,4},{6,5},{7,6},{9,8},{10,9},{11,10},{12... | collective-permute-start | bytes 24584 | tf_op jit(solution)/shard_map/ppermute | solution.py:154

commit v4 on v3

--- a/solution.py
+++ b/solution.py
@@ -54,7 +54,7 @@
         stays = lane >= shift
         for b in range(blocks):
             mixed = jnp.where(stays, lagged_of(c, b), lagged_of(c, b + 1))
-            totals[b] = totals[b] + jnp.take_along_axis(mixed, source, axis=1)
+            totals[b] = totals[b] + jnp.take_along_axis(mixed, source, axis=1, mode="promise_in_bounds")
     return jnp.concatenate(totals, axis=1)
 
 
@@ -75,8 +75,12 @@
         copy.wait()
 
     values = templ_ref[...].astype(f32)
-    centered = values - jnp.mean(values, axis=1, keepdims=True)
-    power = jnp.mean(centered * centered, axis=1, keepdims=True)
+    ones = jnp.ones((tap_count, LANES), jnp.bfloat16)
+    centered = values - jnp.dot(templ_ref[...], ones, preferred_element_type=f32) / tap_count
+    squares = centered * centered
+    high = squares.astype(jnp.bfloat16)
+    low = (squares - high.astype(f32)).astype(jnp.bfloat16)
+    power = (jnp.dot(high, ones, preferred_element_type=f32) + jnp.dot(low, ones, preferred_element_type=f32)) / tap_count
     unit_ref[...] = centered * lax.rsqrt(tap_count * (power + 1e-06))
 
     ext = rec_ref[...].astype(f32)
@@ -88,7 +92,10 @@
     edge_out[:, LANES:LANES + halo_len] = tail_ref[...].astype(f32)
     scale = window_scale(ext, weights, tap_count)
     keep_rolled(ext, rolled_ref)
-    shifts = jnp.transpose(shift_ref[...])
+    shifts = jnp.transpose(shift_ref[...]).astype(f32).astype(jnp.bfloat16)
+    pick = lax.broadcasted_iota(jnp.int32, (chan_count, chan_count * LANES), 1) // LANES
+    pick = (pick == lax.broadcasted_iota(jnp.int32, pick.shape, 0)).astype(f32).astype(jnp.bfloat16)
+    spread_shifts = jnp.dot(shifts, pick, preferred_element_type=f32).astype(jnp.int32)
     for c in range(chan_count):
         lagged = lag_matrix(rolled_ref, c, chan_count, tap_count, lag_count)
         unit = unit_ref[pl.ds(c, templ_count, stride=chan_count), :].astype(jnp.bfloat16)
@@ -96,7 +103,7 @@
         product = jnp.dot(unit, lagged, preferred_element_type=f32) * scale[c:c + 1, :lag_count]
         prod_ref[c] = product
         border_out[c] = product[:, lag_count - LANES:]
-        shift_out[c] = jnp.broadcast_to(shifts[:, c:c + 1], (templ_count, LANES))
+        shift_out[c] = spread_shifts[:, c * LANES:(c + 1) * LANES]
     for k in range(0, templ_count, ROWS):
         halves = [aligned_sum(lambda c: shift_out[c, r:r + 8, :],
                               lambda c, b: prod_ref[c, r:r + 8, b * LANES:(b + 1) * LANES],

time: 26.5 us -> 25.6 us (0.966)
  Pallas kernels: 4.72 us -> 3.78 us
    pallas_call x1, Pallas kernels: 3.41 us -> 2.47 us  [shards(): pl.pallas_call(early_kernel, out_shape=(jax.ShapeDtypeStruct((chan_count,...]
  transfers between devices with their start and end apart: 1 -> 1, of which waited for: 0 -> 0; matrix products, arithmetic and copies ran while one was open for 0% -> 0% of each run, Pallas kernels for 13% -> 10%
where the time goes in v4:
time: 25.6 us; the launch traced here: 25.4 us
  blocking collectives  14.8 us (58%)
  starting transfers between devices  5.9 us (23%)
  Pallas kernels  3.78 us (15%)
  other arithmetic  0.84 us (3%)
    all_to_all x1, blocking collectives, shards(): lax.all_to_all(tiles, 'chan', split_axis=0, concat_axis=0, tiled=True)  14.8 us
    ppermute x1, starting transfers between devices, shards(): nxt = lax.ppermute(record, 'tm', [(i, i - 1) for i in range(1, size)])  5.9 us
    pallas_call x1, Pallas kernels, shards(): pl.pallas_call(early_kernel, out_shape=(jax.ShapeDtypeStruct((chan_count,...  2.47 us
    pallas_call x1, Pallas kernels, shards(): pl.pallas_call(lambda *refs: late_kernel('tm', *refs), out_shape=jax.Shap...  1.31 us
    mul x1, other arithmetic, shards(): return summed[:, :out_len] * jnp.sqrt(tap_count / count)  0.69 us
  transfers between devices with their start and end apart: 1, of which 0 were waited for; matrix products, arithmetic and copies ran while one was open for 0% of the time, Pallas kernels for 10%

profile of v4, /device:TPU:2, one launch (start us, length us, event | category | flops | bytes accessed | tf_op | source)
XLA Modules:
  0.0 25.4 jit_solution(4743151566406847489)
XLA Ops:
  0.0 5.9 %collective-permute-start = (bf16[8,512]{1,0:T(8,128)(2,1)}, bf16[8,512]{1,0:T(8,128)(2,1)S(1)}, u32[]{:S(2)}, u32[]{:S(2)}) collective-permute-start(bf16[8,512]{1,0:T(8,128)(2,1)} %rec_hbm.1), channel_id=1, source_target_pairs={{1,0},{2,1},{3,2},{4,3},{5,4},{6,5},{7,6},{9,8},{10,9},{11,10},{12... | collective-permute-start | bytes 24584 | tf_op jit(solution)/shard_map/ppermute | solution.py:161
  5.9 2.5 %early_lags.1 = (bf16[8,128,128]{2,1,0:T(8,128)(2,1)S(1)}, s32[8,128,128]{2,1,0:T(8,128)S(1)}, f32[8,128,128]{2,1,0:T(8,128)S(1)}, bf16[128,256]{1,0:T(8,128)(2,...) custom-call(bf16[8,512]{1,0:T(8,128)(2,1)} %rec_hbm.1, bf16[8,255]{1,0:T(8,128)(2,1)} %tail_hbm.1, ...), custom_call_target="tpu_custom_call" | custom-call | flops 200000000 | bytes 2000000 | tf_op jit(solution)/shard_map/early_lags/pallas_call | solution.py:162
  8.4 0.0 collective-permute-done.refs_0_
  8.4 1.3 %late_lags.1 = bf16[128,640]{1,0:T(8,128)(2,1)S(1)} custom-call(bf16[8,512]{1,0:T(8,128)(2,1)S(1)} %collective-permute-done.refs_0_, f32[8,384]{1,0:T(8,128)S(1)} %get-tuple-element.11.refs_1_, f32[8,128]{1,0:T(8,128)S(1)} %get-tuple-element.12.refs_2_, bf16[8,128,128]{2,1,0:T(8,128)(2,1)S(1)} %get-tuple-element.13.refs_3_, ...), custom_call_target="tpu_custom_call" | custom-call | tf_op jit(solution)/shard_map/late_lags/pallas_call | solution.py:190
  9.7 14.8 %all_to_all.5 = bf16[16,8,640]{2,1,0:T(8,128)(2,1)S(1)} all-to-all(bf16[16,8,640]{2,1,0:T(8,128)(2,1)S(1)} %bitcast.4), channel_id=1, replica_groups=mesh['chan'=16,'tm'=8] {'chan'}, dimensions={0} | all-to-all | bytes 327680 | tf_op jit(solution)/shard_map/all_to_all | solution.py:204
  24.6 0.1 fusion.2
  24.7 0.7 %slice_multiply_fusion = f32[8,512]{1,0:T(8,128)} fusion(f32[8,640]{1,0:T(8,128)S(1)} %convert_reduce_fusion, f32[8]{0:T(128)S(1)} %fusion.2), kind=kLoop, calls=%fused_computation.1 | loop fusion | flops 4096 | bytes 32800 | tf_op jit(solution)/shard_map/mul | solution.py:207
  (1 shorter events, 0.0 us)
Async XLA Ops:
  0.0 8.4 %collective-permute-start = (bf16[8,512]{1,0:T(8,128)(2,1)}, bf16[8,512]{1,0:T(8,128)(2,1)S(1)}, u32[]{:S(2)}, u32[]{:S(2)}) collective-permute-start(bf16[8,512]{1,0:T(8,128)(2,1)} %rec_hbm.1), channel_id=1, source_target_pairs={{1,0},{2,1},{3,2},{4,3},{5,4},{6,5},{7,6},{9,8},{10,9},{11,10},{12... | collective-permute-start | bytes 24584 | tf_op jit(solution)/shard_map/ppermute | solution.py:161

commit v5 on v4

--- a/solution.py
+++ b/solution.py
@@ -59,7 +59,7 @@
 
 
 def early_kernel(rec_hbm, tail_hbm, templ_hbm, shift_hbm, mask_hbm,
-                 unit_out, shift_out, border_out, first_out, edge_out, weight_out,
+                 unit_out, shift_out, border_out, first_out, edge_out, weight_out, band_out,
                  rec_ref, tail_ref, templ_ref, shift_ref, mask_ref, unit_ref, rolled_ref, prod_ref, sems):
     f32 = jnp.float32
     chan_count = rec_ref.shape[0]
@@ -85,6 +85,8 @@
 
     ext = rec_ref[...].astype(f32)
     weights = jnp.transpose(mask_ref[...]).astype(f32)
+    span = lax.broadcasted_iota(jnp.int32, band_out.shape, 0) - lax.broadcasted_iota(jnp.int32, band_out.shape, 1)
+    band_out[...] = jnp.where((span >= 0) & (span < tap_count), 1.0, 0.0).astype(jnp.bfloat16)
     weight_out[...] = jnp.broadcast_to(weights, (chan_count, LANES))
     halo_len = tail_ref.shape[1]
     edge_out[...] = jnp.zeros(edge_out.shape, f32)
@@ -111,7 +113,7 @@
         first_out[k:k + ROWS, :] = jnp.concatenate(halves, axis=0).astype(jnp.bfloat16)
 
 
-def late_kernel(axis, nxt_ref, edge_ref, weight_ref, unit_ref, shift_ref, border_ref, first_ref, out_ref,
+def late_kernel(axis, nxt_ref, edge_ref, weight_ref, unit_ref, shift_ref, border_ref, first_ref, band_ref, out_ref,
                 ext_ref, rolled_ref, prod_ref):
     f32 = jnp.float32
     chan_count = nxt_ref.shape[0]
@@ -129,7 +131,13 @@
 
     ext = ext_ref[...]
     weights = weight_ref[...]
-    scale = window_scale(ext, weights[:, :1], tap_count)
+    squares = ext * ext
+    high = squares.astype(jnp.bfloat16).astype(f32)
+    stacked = jnp.concatenate([ext, high, squares - high, jnp.zeros_like(ext)], axis=0).astype(jnp.bfloat16)
+    totals = jnp.dot(stacked, band_ref[...], preferred_element_type=f32)
+    window = totals[:chan_count]
+    power = totals[chan_count:2 * chan_count] + totals[2 * chan_count:3 * chan_count]
+    scale = weights[:, :1] * lax.rsqrt(power - window * window / tap_count + tap_count * 1e-06)
     keep_rolled(ext, rolled_ref)
     for c in range(chan_count):
         lagged = lag_matrix(rolled_ref, c, chan_count, tap_count, lag_count)
@@ -159,7 +167,7 @@
     size = lax.axis_size("tm")
     mask_row = mask.reshape(1, chan_count)
     nxt = lax.ppermute(record, "tm", [(i, i - 1) for i in range(1, size)])
-    unit, moved, border, first, edge, weights = pl.pallas_call(
+    unit, moved, border, first, edge, weights, band = pl.pallas_call(
         early_kernel,
         out_shape=(
             jax.ShapeDtypeStruct((chan_count, templ_count, tap_count), bf16),
@@ -168,9 +176,10 @@
             jax.ShapeDtypeStruct((templ_count, first_len), bf16),
             jax.ShapeDtypeStruct((chan_count, 3 * LANES), f32),
             jax.ShapeDtypeStruct((chan_count, LANES), f32),
+            jax.ShapeDtypeStruct((3 * LANES, 2 * LANES), bf16),
         ),
         in_specs=[hbm] * 5,
-        out_specs=(vmem,) * 6,
+        out_specs=(vmem,) * 7,
         scratch_shapes=[
             pltpu.VMEM((chan_count, out_len), bf16),
             pltpu.VMEM(tail.shape, bf16),
@@ -190,7 +199,7 @@
     partial = pl.pallas_call(
         lambda *refs: late_kernel("tm", *refs),
         out_shape=jax.ShapeDtypeStruct((templ_count, out_len + LANES), bf16),
-        in_specs=[vmem] * 7,
+        in_specs=[vmem] * 8,
         out_specs=vmem,
         scratch_shapes=[
             pltpu.VMEM((chan_count, 3 * LANES), f32),
@@ -199,7 +208,7 @@
         ],
         compiler_params=params,
         name="late_lags",
-    )(nxt, edge, weights, unit, moved, border, first)
+    )(nxt, edge, weights, unit, moved, border, first, band)
     tiles = partial.reshape(lax.axis_size("chan"), -1, partial.shape[1])
     arrived = lax.all_to_all(tiles, "chan", split_axis=0, concat_axis=0, tiled=True)
     summed = jnp.sum(arrived.astype(f32), axis=0)

time: 25.6 us -> 25.4 us (level)
  no operation moved by 1% of the time
where the time goes in v5:
time: 25.4 us; the launch traced here: 25.2 us
  blocking collectives  14.8 us (58%)
  starting transfers between devices  5.9 us (23%)
  Pallas kernels  3.63 us (14%)
  other arithmetic  0.84 us (3%)
    all_to_all x1, blocking collectives, shards(): lax.all_to_all(tiles, 'chan', split_axis=0, concat_axis=0, tiled=True)  14.8 us
    ppermute x1, starting transfers between devices, shards(): nxt = lax.ppermute(record, 'tm', [(i, i - 1) for i in range(1, size)])  5.9 us
    pallas_call x1, Pallas kernels, shards(): pl.pallas_call(early_kernel, out_shape=(jax.ShapeDtypeStruct((chan_count,...  2.51 us
    pallas_call x1, Pallas kernels, shards(): pl.pallas_call(lambda *refs: late_kernel('tm', *refs), out_shape=jax.Shap...  1.12 us
    mul x1, other arithmetic, shards(): return summed[:, :out_len] * jnp.sqrt(tap_count / count)  0.69 us
  transfers between devices with their start and end apart: 1, of which 0 were waited for; matrix products, arithmetic and copies ran while one was open for 0% of the time, Pallas kernels for 10%

profile of v5, /device:TPU:2, one launch (start us, length us, event | category | flops | bytes accessed | tf_op | source)
XLA Modules:
  0.0 25.2 jit_solution(15143303630090163634)
XLA Ops:
  0.0 5.9 %collective-permute-start = (bf16[8,512]{1,0:T(8,128)(2,1)}, bf16[8,512]{1,0:T(8,128)(2,1)S(1)}, u32[]{:S(2)}, u32[]{:S(2)}) collective-permute-start(bf16[8,512]{1,0:T(8,128)(2,1)} %rec_hbm.1), channel_id=1, source_target_pairs={{1,0},{2,1},{3,2},{4,3},{5,4},{6,5},{7,6},{9,8},{10,9},{11,10},{12... | collective-permute-start | bytes 24584 | tf_op jit(solution)/shard_map/ppermute | solution.py:169
  5.9 2.5 %early_lags.1 = (bf16[8,128,128]{2,1,0:T(8,128)(2,1)S(1)}, s32[8,128,128]{2,1,0:T(8,128)S(1)}, f32[8,128,128]{2,1,0:T(8,128)S(1)}, bf16[128,256]{1,0:T(8,128)(2,...) custom-call(bf16[8,512]{1,0:T(8,128)(2,1)} %rec_hbm.1, bf16[8,255]{1,0:T(8,128)(2,1)} %tail_hbm.1, ...), custom_call_target="tpu_custom_call" | custom-call | flops 200000000 | bytes 2000000 | tf_op jit(solution)/shard_map/early_lags/pallas_call | solution.py:170
  8.4 0.0 collective-permute-done.refs_0_
  8.4 1.1 %late_lags.1 = bf16[128,640]{1,0:T(8,128)(2,1)S(1)} custom-call(bf16[8,512]{1,0:T(8,128)(2,1)S(1)} %collective-permute-done.refs_0_, f32[8,384]{1,0:T(8,128)S(1)} %get-tuple-element.12.refs_1_, f32[8,128]{1,0:T(8,128)S(1)} %get-tuple-element.13.refs_2_, bf16[8,128,128]{2,1,0:T(8,128)(2,1)S(1)} %get-tuple-element.14.refs_3_, ...), custom_call_target="tpu_custom_call" | custom-call | tf_op jit(solution)/shard_map/late_lags/pallas_call | solution.py:199
  9.6 14.8 %all_to_all.5 = bf16[16,8,640]{2,1,0:T(8,128)(2,1)S(1)} all-to-all(bf16[16,8,640]{2,1,0:T(8,128)(2,1)S(1)} %bitcast.4), channel_id=1, replica_groups=mesh['chan'=16,'tm'=8] {'chan'}, dimensions={0} | all-to-all | bytes 327680 | tf_op jit(solution)/shard_map/all_to_all | solution.py:213
  24.4 0.1 fusion.2
  24.5 0.7 %slice_multiply_fusion = f32[8,512]{1,0:T(8,128)} fusion(f32[8,640]{1,0:T(8,128)S(1)} %convert_reduce_fusion, f32[8]{0:T(128)S(1)} %fusion.2), kind=kLoop, calls=%fused_computation.1 | loop fusion | flops 4096 | bytes 32800 | tf_op jit(solution)/shard_map/mul | solution.py:216
  (1 shorter events, 0.0 us)
Async XLA Ops:
  0.0 8.4 %collective-permute-start = (bf16[8,512]{1,0:T(8,128)(2,1)}, bf16[8,512]{1,0:T(8,128)(2,1)S(1)}, u32[]{:S(2)}, u32[]{:S(2)}) collective-permute-start(bf16[8,512]{1,0:T(8,128)(2,1)} %rec_hbm.1), channel_id=1, source_target_pairs={{1,0},{2,1},{3,2},{4,3},{5,4},{6,5},{7,6},{9,8},{10,9},{11,10},{12... | collective-permute-start | bytes 24584 | tf_op jit(solution)/shard_map/ppermute | solution.py:169

commit v6 on v4

--- a/solution.py
+++ b/solution.py
@@ -58,8 +58,20 @@
     return jnp.concatenate(totals, axis=1)
 
 
+def band_scale(ext, weights, band, tap_count):
+    f32 = jnp.float32
+    chan_count = ext.shape[0]
+    squares = ext * ext
+    high = squares.astype(jnp.bfloat16).astype(f32)
+    stacked = jnp.concatenate([ext, high, squares - high, jnp.zeros_like(ext)], axis=0).astype(jnp.bfloat16)
+    totals = jnp.dot(stacked, band, preferred_element_type=f32)
+    window = totals[:chan_count]
+    power = totals[chan_count:2 * chan_count] + totals[2 * chan_count:3 * chan_count]
+    return weights * lax.rsqrt(power - window * window / tap_count + tap_count * 1e-06)
+
+
 def early_kernel(rec_hbm, tail_hbm, templ_hbm, shift_hbm, mask_hbm,
-                 unit_out, shift_out, border_out, first_out, edge_out, weight_out,
+                 unit_out, shift_out, border_out, first_out, edge_out, weight_out, band_out,
                  rec_ref, tail_ref, templ_ref, shift_ref, mask_ref, unit_ref, rolled_ref, prod_ref, sems):
     f32 = jnp.float32
     chan_count = rec_ref.shape[0]
@@ -85,12 +97,16 @@
 
     ext = rec_ref[...].astype(f32)
     weights = jnp.transpose(mask_ref[...]).astype(f32)
+    shape = (ext.shape[1], lag_count)
+    span = lax.broadcasted_iota(jnp.int32, shape, 0) - lax.broadcasted_iota(jnp.int32, shape, 1)
+    band_all = jnp.where((span >= 0) & (span < tap_count), 1.0, 0.0).astype(jnp.bfloat16)
+    band_out[...] = band_all[:band_out.shape[0], :band_out.shape[1]]
     weight_out[...] = jnp.broadcast_to(weights, (chan_count, LANES))
     halo_len = tail_ref.shape[1]
     edge_out[...] = jnp.zeros(edge_out.shape, f32)
     edge_out[:, :LANES] = ext[:, ext.shape[1] - LANES:]
     edge_out[:, LANES:LANES + halo_len] = tail_ref[...].astype(f32)
-    scale = window_scale(ext, weights, tap_count)
+    scale = band_scale(ext, weights, band_all, tap_count)
     keep_rolled(ext, rolled_ref)
     shifts = jnp.transpose(shift_ref[...]).astype(f32).astype(jnp.bfloat16)
     pick = lax.broadcasted_iota(jnp.int32, (chan_count, chan_count * LANES), 1) // LANES
@@ -111,26 +127,32 @@
         first_out[k:k + ROWS, :] = jnp.concatenate(halves, axis=0).astype(jnp.bfloat16)
 
 
-def late_kernel(axis, nxt_ref, edge_ref, weight_ref, unit_ref, shift_ref, border_ref, first_ref, out_ref,
+def late_kernel(axis, even_ref, odd_ref, edge_ref, weight_ref, unit_ref, shift_ref, border_ref, first_ref, band_ref, out_ref,
                 ext_ref, rolled_ref, prod_ref):
     f32 = jnp.float32
-    chan_count = nxt_ref.shape[0]
+    chan_count = even_ref.shape[0]
     templ_count, first_len = first_ref.shape
     tap_count = unit_ref.shape[2]
     lag_count = prod_ref.shape[2]
     blocks = lag_count // LANES
     out_len = first_len + lag_count
-    at_end = lax.axis_index(axis) == lax.axis_size(axis) - 1
+    place = lax.axis_index(axis)
+    at_end = place == lax.axis_size(axis) - 1
+    is_odd = lax.rem(place, 2) == 1
     ext_ref[...] = edge_ref[...]
 
-    @pl.when(jnp.logical_not(at_end))
+    @pl.when(jnp.logical_not(is_odd))
     def _():
-        ext_ref[:, LANES:] = nxt_ref[:, :2 * LANES].astype(f32)
+        ext_ref[:, LANES:] = even_ref[:, :2 * LANES].astype(f32)
+
+    @pl.when(jnp.logical_and(is_odd, jnp.logical_not(at_end)))
+    def _():
+        ext_ref[:, LANES:] = odd_ref[:, :2 * LANES].astype(f32)
 
     ext = ext_ref[...]
     weights = weight_ref[...]
-    scale = window_scale(ext, weights[:, :1], tap_count)
     keep_rolled(ext, rolled_ref)
+    scale = band_scale(ext, weights[:, :1], band_ref[...], tap_count)
     for c in range(chan_count):
         lagged = lag_matrix(rolled_ref, c, chan_count, tap_count, lag_count)
         prod_ref[c] = jnp.dot(unit_ref[c], lagged, preferred_element_type=f32) * scale[c:c + 1, :lag_count]
@@ -158,8 +180,16 @@
     params = pltpu.CompilerParams(vmem_limit_bytes=VMEM_BYTES)
     size = lax.axis_size("tm")
     mask_row = mask.reshape(1, chan_count)
-    nxt = lax.ppermute(record, "tm", [(i, i - 1) for i in range(1, size)])
-    unit, moved, border, first, edge, weights = pl.pallas_call(
+    even_odd = [(i, i ^ 1) for i in range(size)]
+    ends = (0, size - 1)
+    odd_even = []
+    for group in range(lax.axis_size("chan")):
+        for i in range(size):
+            to = (group ^ 1, i) if i in ends else (group, ((i - 1) ^ 1) + 1)
+            odd_even.append((group * size + i, to[0] * size + to[1]))
+    to_even = lax.ppermute(record, "tm", even_odd)
+    to_odd = lax.ppermute(record, ("chan", "tm"), odd_even)
+    unit, moved, border, first, edge, weights, band = pl.pallas_call(
         early_kernel,
         out_shape=(
             jax.ShapeDtypeStruct((chan_count, templ_count, tap_count), bf16),
@@ -168,9 +198,10 @@
             jax.ShapeDtypeStruct((templ_count, first_len), bf16),
             jax.ShapeDtypeStruct((chan_count, 3 * LANES), f32),
             jax.ShapeDtypeStruct((chan_count, LANES), f32),
+            jax.ShapeDtypeStruct((3 * LANES, 2 * LANES), bf16),
         ),
         in_specs=[hbm] * 5,
-        out_specs=(vmem,) * 6,
+        out_specs=(vmem,) * 7,
         scratch_shapes=[
             pltpu.VMEM((chan_count, out_len), bf16),
             pltpu.VMEM(tail.shape, bf16),
@@ -190,7 +221,7 @@
     partial = pl.pallas_call(
         lambda *refs: late_kernel("tm", *refs),
         out_shape=jax.ShapeDtypeStruct((templ_count, out_len + LANES), bf16),
-        in_specs=[vmem] * 7,
+        in_specs=[vmem] * 9,
         out_specs=vmem,
         scratch_shapes=[
             pltpu.VMEM((chan_count, 3 * LANES), f32),
@@ -199,7 +230,7 @@
         ],
         compiler_params=params,
         name="late_lags",
-    )(nxt, edge, weights, unit, moved, border, first)
+    )(to_even, to_odd, edge, weights, unit, moved, border, first, band)
     tiles = partial.reshape(lax.axis_size("chan"), -1, partial.shape[1])
     arrived = lax.all_to_all(tiles, "chan", split_axis=0, concat_axis=0, tiled=True)
     summed = jnp.sum(arrived.astype(f32), axis=0)

time: 25.6 us -> 24.5 us (0.957)
  starting transfers between devices: 5.9 us -> 4.41 us
  waiting for transfers between devices: 0.01 us -> 1.04 us
  blocking collectives: 14.8 us -> 14.5 us
    ppermute x1 -> x2, starting transfers between devices: 5.9 us -> 4.41 us  [the longest x1 2.49 us: shards(): to_odd = lax.ppermute(record, ('chan', 'tm'), odd_even)]
    ppermute x1 -> x2, waiting for transfers between devices: 0.01 us -> 1.04 us  [the longest x1 1.04 us: shards(): to_odd = lax.ppermute(record, ('chan', 'tm'), odd_even)]
    all_to_all x1, blocking collectives: 14.8 us -> 14.5 us  [shards(): lax.all_to_all(tiles, 'chan', split_axis=0, concat_axis=0, tiled=True)]
  transfers between devices with their start and end apart: 1 -> 2, of which waited for: 0 -> 1; matrix products, arithmetic and copies ran while one was open for 0% -> 0% of each run, Pallas kernels for 10% -> 10%
where the time goes in v6:
time: 24.5 us; the launch traced here: 24.4 us
  blocking collectives  14.5 us (59%)
  starting transfers between devices  4.41 us (18%)
  Pallas kernels  3.53 us (14%)
  waiting for transfers between devices  1.04 us (4%)
  other arithmetic  0.84 us (3%)
    all_to_all x1, blocking collectives, shards(): lax.all_to_all(tiles, 'chan', split_axis=0, concat_axis=0, tiled=True)  14.5 us
    ppermute x1, starting transfers between devices, shards(): to_odd = lax.ppermute(record, ('chan', 'tm'), odd_even)  2.49 us
    pallas_call x1, Pallas kernels, shards(): pl.pallas_call(early_kernel, out_shape=(jax.ShapeDtypeStruct((chan_count,...  2.42 us
    ppermute x1, starting transfers between devices, shards(): to_even = lax.ppermute(record, 'tm', even_odd)  1.92 us
    pallas_call x1, Pallas kernels, shards(): pl.pallas_call(lambda *refs: late_kernel('tm', *refs), out_shape=jax.Shap...  1.11 us
    ppermute x1, waiting for transfers between devices, shards(): to_odd = lax.ppermute(record, ('chan', 'tm'), odd_even)  1.04 us
    mul x1, other arithmetic, shards(): return summed[:, :out_len] * jnp.sqrt(tap_count / count)  0.69 us
  transfers between devices with their start and end apart: 2, of which 1 were waited for; matrix products, arithmetic and copies ran while one was open for 0% of the time, Pallas kernels for 10%

profile of v6, /device:TPU:2, one launch (start us, length us, event | category | flops | bytes accessed | tf_op | source)
XLA Modules:
  0.0 24.4 jit_solution(6983058711214958025)
XLA Ops:
  0.0 1.9 %collective-permute-start = (bf16[8,512]{1,0:T(8,128)(2,1)}, bf16[8,512]{1,0:T(8,128)(2,1)S(1)}, u32[]{:S(2)}, u32[]{:S(2)}) collective-permute-start(bf16[8,512]{1,0:T(8,128)(2,1)} %rec_hbm.1), channel_id=1, source_target_pairs={{0,1},{1,0},{2,3},{3,2},{4,5},{5,4},{6,7},{7,6},{8,9},{9,8},{10,11... | collective-permute-start | bytes 24584 | tf_op jit(solution)/shard_map/ppermute | solution.py:190
  1.9 2.5 %collective-permute-start.1 = (bf16[8,512]{1,0:T(8,128)(2,1)}, bf16[8,512]{1,0:T(8,128)(2,1)S(1)}, u32[]{:S(2)}, u32[]{:S(2)}) collective-permute-start(bf16[8,512]{1,0:T(8,128)(2,1)} %rec_hbm.1), channel_id=1, source_target_pairs={{0,8},{1,2},{2,1},{3,4},{4,3},{5,6},{6,5},{7,15},{8,0},{9,10},{10,... | collective-permute-start | bytes 24584 | tf_op jit(solution)/shard_map/ppermute | solution.py:191
  4.4 2.4 %early_lags.1 = (bf16[8,128,128]{2,1,0:T(8,128)(2,1)S(1)}, s32[8,128,128]{2,1,0:T(8,128)S(1)}, f32[8,128,128]{2,1,0:T(8,128)S(1)}, bf16[128,256]{1,0:T(8,128)(2,...) custom-call(bf16[8,512]{1,0:T(8,128)(2,1)} %rec_hbm.1, bf16[8,255]{1,0:T(8,128)(2,1)} %tail_hbm.1, ...), custom_call_target="tpu_custom_call" | custom-call | flops 200000000 | bytes 2000000 | tf_op jit(solution)/shard_map/early_lags/pallas_call | solution.py:192
  6.8 0.0 collective-permute-done.refs_0_
  6.9 1.0 %collective-permute-done.1.refs_1_ = bf16[8,512]{1,0:T(8,128)(2,1)S(1)} collective-permute-done((bf16[8,512]{1,0:T(8,128)(2,1)}, bf16[8,512]{1,0:T(8,128)(2,1)S(1)}, u32[]{:S(2)}, u32[]{:S(2)}) %collective-permute-start.1) | collective-permute-done | bytes 8224 | tf_op jit(solution)/shard_map/ppermute | solution.py:191
  7.9 1.1 %late_lags.1 = bf16[128,640]{1,0:T(8,128)(2,1)S(1)} custom-call(bf16[8,512]{1,0:T(8,128)(2,1)S(1)} %collective-permute-done.refs_0_, bf16[8,512]{1,0:T(8,128)(2,1)S(1)} %collective-permute-done.1.refs_1_, f32[8,384]{1,0:T(8,128)S(1)} %get-tuple-element.12.refs_2_, f32[8,128]{1,0:T(8,128)S(1)} %get-tuple-element.13.refs_3_, ...), custom_call_target="tpu_custom_call" | custom-call | tf_op jit(solution)/shard_map/late_lags/pallas_call | solution.py:221
  9.0 14.5 %all_to_all.5 = bf16[16,8,640]{2,1,0:T(8,128)(2,1)S(1)} all-to-all(bf16[16,8,640]{2,1,0:T(8,128)(2,1)S(1)} %bitcast.4), channel_id=1, replica_groups=mesh['chan'=16,'tm'=8] {'chan'}, dimensions={0} | all-to-all | bytes 327680 | tf_op jit(solution)/shard_map/all_to_all | solution.py:235
  23.5 0.1 fusion.2
  23.7 0.7 %slice_multiply_fusion = f32[8,512]{1,0:T(8,128)} fusion(f32[8,640]{1,0:T(8,128)S(1)} %convert_reduce_fusion, f32[8]{0:T(128)S(1)} %fusion.2), kind=kLoop, calls=%fused_computation.1 | loop fusion | flops 4096 | bytes 32800 | tf_op jit(solution)/shard_map/mul | solution.py:238
  (1 shorter events, 0.0 us)
Async XLA Ops:
  0.0 6.8 %collective-permute-start = (bf16[8,512]{1,0:T(8,128)(2,1)}, bf16[8,512]{1,0:T(8,128)(2,1)S(1)}, u32[]{:S(2)}, u32[]{:S(2)}) collective-permute-start(bf16[8,512]{1,0:T(8,128)(2,1)} %rec_hbm.1), channel_id=1, source_target_pairs={{0,1},{1,0},{2,3},{3,2},{4,5},{5,4},{6,7},{7,6},{8,9},{9,8},{10,11... | collective-permute-start | bytes 24584 | tf_op jit(solution)/shard_map/ppermute | solution.py:190
  1.9 6.0 %collective-permute-start.1 = (bf16[8,512]{1,0:T(8,128)(2,1)}, bf16[8,512]{1,0:T(8,128)(2,1)S(1)}, u32[]{:S(2)}, u32[]{:S(2)}) collective-permute-start(bf16[8,512]{1,0:T(8,128)(2,1)} %rec_hbm.1), channel_id=1, source_target_pairs={{0,8},{1,2},{2,1},{3,4},{4,3},{5,6},{6,5},{7,15},{8,0},{9,10},{10,... | collective-permute-start | bytes 24584 | tf_op jit(solution)/shard_map/ppermute | solution.py:191

commit v7 on v6

--- a/solution.py
+++ b/solution.py
@@ -127,6 +127,25 @@
         first_out[k:k + ROWS, :] = jnp.concatenate(halves, axis=0).astype(jnp.bfloat16)
 
 
+def aligned_half(place, lagged_of, blocks, chan_count):
+    lane = lax.broadcasted_iota(jnp.int32, (ROWS, LANES), 1)
+    totals = [jnp.zeros((ROWS, LANES), jnp.float32)] * blocks
+    for c in range(chan_count):
+        shift = place(c)
+        source = ((lane + shift) & (LANES - 1)).astype(jnp.int16)
+        stays = lane >= shift
+        for b in range(blocks):
+            mixed = jnp.where(stays, lagged_of(c, b), lagged_of(c, b + 1)).astype(jnp.bfloat16)
+            moved = lax.gather(
+                mixed, source[:, :, None],
+                lax.GatherDimensionNumbers(
+                    offset_dims=(), collapsed_slice_dims=(1,), start_index_map=(1,),
+                    operand_batching_dims=(0,), start_indices_batching_dims=(0,)),
+                (1, 1), mode=lax.GatherScatterMode.PROMISE_IN_BOUNDS)
+            totals[b] = totals[b] + moved.astype(jnp.float32)
+    return jnp.concatenate(totals, axis=1)
+
+
 def late_kernel(axis, even_ref, odd_ref, edge_ref, weight_ref, unit_ref, shift_ref, border_ref, first_ref, band_ref, out_ref,
                 ext_ref, rolled_ref, prod_ref):
     f32 = jnp.float32
@@ -158,12 +177,11 @@
         prod_ref[c] = jnp.dot(unit_ref[c], lagged, preferred_element_type=f32) * scale[c:c + 1, :lag_count]
     for k in range(0, templ_count, ROWS):
         def lagged_of(c, b):
-            rows = slice(r, r + 8)
+            rows = slice(r, r + ROWS)
             return border_ref[c, rows, :] if b == 0 else prod_ref[c, rows, (b - 1) * LANES:b * LANES]
-        halves = []
-        for r in (k, k + 8):
-            halves.append(aligned_sum(lambda c: shift_ref[c, r:r + 8, :], lagged_of, blocks, chan_count))
-        out_ref[k:k + ROWS, first_len:out_len] = jnp.concatenate(halves, axis=0).astype(jnp.bfloat16)
+        r = k
+        both = aligned_half(lambda c: shift_ref[c, k:k + ROWS, :], lagged_of, blocks, chan_count)
+        out_ref[k:k + ROWS, first_len:out_len] = both.astype(jnp.bfloat16)
     out_ref[:, :first_len] = first_ref[...]
     count = jnp.sum(weights, axis=0, keepdims=True)
     out_ref[:, out_len:] = jnp.broadcast_to(count, (templ_count, LANES)).astype(jnp.bfloat16)

time: 24.5 us -> 24.2 us (0.988)
  Pallas kernels: 3.53 us -> 3.22 us
    pallas_call x1, Pallas kernels: 1.11 us -> 0.8 us  [shards(): pl.pallas_call(lambda *refs: late_kernel('tm', *refs), out_shape=jax.Shap...]
where the time goes in v7:
time: 24.2 us; the launch traced here: 24 us
  blocking collectives  14.5 us (60%)
  starting transfers between devices  4.41 us (18%)
  Pallas kernels  3.22 us (13%)
  waiting for transfers between devices  1.04 us (4%)
  other arithmetic  0.84 us (3%)
    all_to_all x1, blocking collectives, shards(): lax.all_to_all(tiles, 'chan', split_axis=0, concat_axis=0, tiled=True)  14.5 us
    ppermute x1, starting transfers between devices, shards(): to_odd = lax.ppermute(record, ('chan', 'tm'), odd_even)  2.49 us
    pallas_call x1, Pallas kernels, shards(): pl.pallas_call(early_kernel, out_shape=(jax.ShapeDtypeStruct((chan_count,...  2.42 us
    ppermute x1, starting transfers between devices, shards(): to_even = lax.ppermute(record, 'tm', even_odd)  1.92 us
    ppermute x1, waiting for transfers between devices, shards(): to_odd = lax.ppermute(record, ('chan', 'tm'), odd_even)  1.04 us
    pallas_call x1, Pallas kernels, shards(): pl.pallas_call(lambda *refs: late_kernel('tm', *refs), out_shape=jax.Shap...  0.8 us
    mul x1, other arithmetic, shards(): return summed[:, :out_len] * jnp.sqrt(tap_count / count)  0.69 us
  transfers between devices with their start and end apart: 2, of which 1 were waited for; matrix products, arithmetic and copies ran while one was open for 0% of the time, Pallas kernels for 10%

profile of v7, /device:TPU:2, one launch (start us, length us, event | category | flops | bytes accessed | tf_op | source)
XLA Modules:
  0.0 24.0 jit_solution(7029328045601854144)
XLA Ops:
  0.0 1.9 %collective-permute-start = (bf16[8,512]{1,0:T(8,128)(2,1)}, bf16[8,512]{1,0:T(8,128)(2,1)S(1)}, u32[]{:S(2)}, u32[]{:S(2)}) collective-permute-start(bf16[8,512]{1,0:T(8,128)(2,1)} %rec_hbm.1), channel_id=1, source_target_pairs={{0,1},{1,0},{2,3},{3,2},{4,5},{5,4},{6,7},{7,6},{8,9},{9,8},{10,11... | collective-permute-start | bytes 24584 | tf_op jit(solution)/shard_map/ppermute | solution.py:208
  1.9 2.5 %collective-permute-start.1 = (bf16[8,512]{1,0:T(8,128)(2,1)}, bf16[8,512]{1,0:T(8,128)(2,1)S(1)}, u32[]{:S(2)}, u32[]{:S(2)}) collective-permute-start(bf16[8,512]{1,0:T(8,128)(2,1)} %rec_hbm.1), channel_id=1, source_target_pairs={{0,8},{1,2},{2,1},{3,4},{4,3},{5,6},{6,5},{7,15},{8,0},{9,10},{10,... | collective-permute-start | bytes 24584 | tf_op jit(solution)/shard_map/ppermute | solution.py:209
  4.4 2.4 %early_lags.1 = (bf16[8,128,128]{2,1,0:T(8,128)(2,1)S(1)}, s32[8,128,128]{2,1,0:T(8,128)S(1)}, f32[8,128,128]{2,1,0:T(8,128)S(1)}, bf16[128,256]{1,0:T(8,128)(2,...) custom-call(bf16[8,512]{1,0:T(8,128)(2,1)} %rec_hbm.1, bf16[8,255]{1,0:T(8,128)(2,1)} %tail_hbm.1, ...), custom_call_target="tpu_custom_call" | custom-call | flops 200000000 | bytes 2000000 | tf_op jit(solution)/shard_map/early_lags/pallas_call | solution.py:210
  6.8 0.0 collective-permute-done.refs_0_
  6.9 1.0 %collective-permute-done.1.refs_1_ = bf16[8,512]{1,0:T(8,128)(2,1)S(1)} collective-permute-done((bf16[8,512]{1,0:T(8,128)(2,1)}, bf16[8,512]{1,0:T(8,128)(2,1)S(1)}, u32[]{:S(2)}, u32[]{:S(2)}) %collective-permute-start.1) | collective-permute-done | bytes 8224 | tf_op jit(solution)/shard_map/ppermute | solution.py:209
  7.9 0.8 %late_lags.1 = bf16[128,640]{1,0:T(8,128)(2,1)S(1)} custom-call(bf16[8,512]{1,0:T(8,128)(2,1)S(1)} %collective-permute-done.refs_0_, bf16[8,512]{1,0:T(8,128)(2,1)S(1)} %collective-permute-done.1.refs_1_, f32[8,384]{1,0:T(8,128)S(1)} %get-tuple-element.12.refs_2_, f32[8,128]{1,0:T(8,128)S(1)} %get-tuple-element.13.refs_3_, ...), custom_call_target="tpu_custom_call" | custom-call | tf_op jit(solution)/shard_map/late_lags/pallas_call | solution.py:239
  8.7 14.5 %all_to_all.5 = bf16[16,8,640]{2,1,0:T(8,128)(2,1)S(1)} all-to-all(bf16[16,8,640]{2,1,0:T(8,128)(2,1)S(1)} %bitcast.4), channel_id=1, replica_groups=mesh['chan'=16,'tm'=8] {'chan'}, dimensions={0} | all-to-all | bytes 327680 | tf_op jit(solution)/shard_map/all_to_all | solution.py:253
  23.2 0.1 fusion.2
  23.4 0.7 %slice_multiply_fusion = f32[8,512]{1,0:T(8,128)} fusion(f32[8,640]{1,0:T(8,128)S(1)} %convert_reduce_fusion, f32[8]{0:T(128)S(1)} %fusion.2), kind=kLoop, calls=%fused_computation.1 | loop fusion | flops 4096 | bytes 32800 | tf_op jit(solution)/shard_map/mul | solution.py:256
  (1 shorter events, 0.0 us)
Async XLA Ops:
  0.0 6.8 %collective-permute-start = (bf16[8,512]{1,0:T(8,128)(2,1)}, bf16[8,512]{1,0:T(8,128)(2,1)S(1)}, u32[]{:S(2)}, u32[]{:S(2)}) collective-permute-start(bf16[8,512]{1,0:T(8,128)(2,1)} %rec_hbm.1), channel_id=1, source_target_pairs={{0,1},{1,0},{2,3},{3,2},{4,5},{5,4},{6,7},{7,6},{8,9},{9,8},{10,11... | collective-permute-start | bytes 24584 | tf_op jit(solution)/shard_map/ppermute | solution.py:208
  1.9 6.0 %collective-permute-start.1 = (bf16[8,512]{1,0:T(8,128)(2,1)}, bf16[8,512]{1,0:T(8,128)(2,1)S(1)}, u32[]{:S(2)}, u32[]{:S(2)}) collective-permute-start(bf16[8,512]{1,0:T(8,128)(2,1)} %rec_hbm.1), channel_id=1, source_target_pairs={{0,8},{1,2},{2,1},{3,4},{4,3},{5,6},{6,5},{7,15},{8,0},{9,10},{10,... | collective-permute-start | bytes 24584 | tf_op jit(solution)/shard_map/ppermute | solution.py:209

commit v8 on v7

--- a/solution.py
+++ b/solution.py
@@ -252,8 +252,8 @@
     tiles = partial.reshape(lax.axis_size("chan"), -1, partial.shape[1])
     arrived = lax.all_to_all(tiles, "chan", split_axis=0, concat_axis=0, tiled=True)
     summed = jnp.sum(arrived.astype(f32), axis=0)
-    count = jnp.maximum(summed[:, out_len:out_len + 1], 1.0)
-    return summed[:, :out_len] * jnp.sqrt(tap_count / count)
+    factor = jnp.sqrt(tap_count / jnp.maximum(summed[:, out_len:], 1.0))
+    return jnp.concatenate([summed[:, b:b + LANES] * factor for b in range(0, out_len, LANES)], axis=1)
 
 
 def solution(mesh):

time: 24.2 us -> 24 us (level)
    mul x1, other arithmetic: 0.69 us -> 0.01 us  [shards(): summed[:, b:b + LANES] * factor]
    concatenate x0 -> x1, other arithmetic: none -> 0.62 us  [shards(): jnp.concatenate([summed[:, b:b + LANES] * factor for b in range(0, out_le...]
where the time goes in v8:
time: 24 us; the launch traced here: 23.9 us
  blocking collectives  14.5 us (60%)
  starting transfers between devices  4.41 us (18%)
  Pallas kernels  3.22 us (13%)
  waiting for transfers between devices  1.04 us (4%)
  other arithmetic  0.66 us (3%)
    all_to_all x1, blocking collectives, shards(): lax.all_to_all(tiles, 'chan', split_axis=0, concat_axis=0, tiled=True)  14.5 us
    ppermute x1, starting transfers between devices, shards(): to_odd = lax.ppermute(record, ('chan', 'tm'), odd_even)  2.49 us
    pallas_call x1, Pallas kernels, shards(): pl.pallas_call(early_kernel, out_shape=(jax.ShapeDtypeStruct((chan_count,...  2.42 us
    ppermute x1, starting transfers between devices, shards(): to_even = lax.ppermute(record, 'tm', even_odd)  1.92 us
    ppermute x1, waiting for transfers between devices, shards(): to_odd = lax.ppermute(record, ('chan', 'tm'), odd_even)  1.04 us
    pallas_call x1, Pallas kernels, shards(): pl.pallas_call(lambda *refs: late_kernel('tm', *refs), out_shape=jax.Shap...  0.8 us
    concatenate x1, other arithmetic, shards(): jnp.concatenate([summed[:, b:b + LANES] * factor for b in range(0, out_le...  0.62 us
  transfers between devices with their start and end apart: 2, of which 1 were waited for; matrix products, arithmetic and copies ran while one was open for 0% of the time, Pallas kernels for 10%

profile of v8, /device:TPU:2, one launch (start us, length us, event | category | flops | bytes accessed | tf_op | source)
XLA Modules:
  0.0 23.9 jit_solution(1935840744134511156)
XLA Ops:
  0.0 1.9 %collective-permute-start = (bf16[8,512]{1,0:T(8,128)(2,1)}, bf16[8,512]{1,0:T(8,128)(2,1)S(1)}, u32[]{:S(2)}, u32[]{:S(2)}) collective-permute-start(bf16[8,512]{1,0:T(8,128)(2,1)} %rec_hbm.1), channel_id=1, source_target_pairs={{0,1},{1,0},{2,3},{3,2},{4,5},{5,4},{6,7},{7,6},{8,9},{9,8},{10,11... | collective-permute-start | bytes 24584 | tf_op jit(solution)/shard_map/ppermute | solution.py:208
  1.9 2.5 %collective-permute-start.1 = (bf16[8,512]{1,0:T(8,128)(2,1)}, bf16[8,512]{1,0:T(8,128)(2,1)S(1)}, u32[]{:S(2)}, u32[]{:S(2)}) collective-permute-start(bf16[8,512]{1,0:T(8,128)(2,1)} %rec_hbm.1), channel_id=1, source_target_pairs={{0,8},{1,2},{2,1},{3,4},{4,3},{5,6},{6,5},{7,15},{8,0},{9,10},{10,... | collective-permute-start | bytes 24584 | tf_op jit(solution)/shard_map/ppermute | solution.py:209
  4.4 2.4 %early_lags.1 = (bf16[8,128,128]{2,1,0:T(8,128)(2,1)S(1)}, s32[8,128,128]{2,1,0:T(8,128)S(1)}, f32[8,128,128]{2,1,0:T(8,128)S(1)}, bf16[128,256]{1,0:T(8,128)(2,...) custom-call(bf16[8,512]{1,0:T(8,128)(2,1)} %rec_hbm.1, bf16[8,255]{1,0:T(8,128)(2,1)} %tail_hbm.1, ...), custom_call_target="tpu_custom_call" | custom-call | flops 200000000 | bytes 2000000 | tf_op jit(solution)/shard_map/early_lags/pallas_call | solution.py:210
  6.8 0.0 collective-permute-done.refs_0_
  6.9 1.0 %collective-permute-done.1.refs_1_ = bf16[8,512]{1,0:T(8,128)(2,1)S(1)} collective-permute-done((bf16[8,512]{1,0:T(8,128)(2,1)}, bf16[8,512]{1,0:T(8,128)(2,1)S(1)}, u32[]{:S(2)}, u32[]{:S(2)}) %collective-permute-start.1) | collective-permute-done | bytes 8224 | tf_op jit(solution)/shard_map/ppermute | solution.py:209
  7.9 0.8 %late_lags.1 = bf16[128,640]{1,0:T(8,128)(2,1)S(1)} custom-call(bf16[8,512]{1,0:T(8,128)(2,1)S(1)} %collective-permute-done.refs_0_, bf16[8,512]{1,0:T(8,128)(2,1)S(1)} %collective-permute-done.1.refs_1_, f32[8,384]{1,0:T(8,128)S(1)} %get-tuple-element.12.refs_2_, f32[8,128]{1,0:T(8,128)S(1)} %get-tuple-element.13.refs_3_, ...), custom_call_target="tpu_custom_call" | custom-call | tf_op jit(solution)/shard_map/late_lags/pallas_call | solution.py:239
  8.7 14.5 %all_to_all.5 = bf16[16,8,640]{2,1,0:T(8,128)(2,1)S(1)} all-to-all(bf16[16,8,640]{2,1,0:T(8,128)(2,1)S(1)} %bitcast.4), channel_id=1, replica_groups=mesh['chan'=16,'tm'=8] {'chan'}, dimensions={0} | all-to-all | bytes 327680 | tf_op jit(solution)/shard_map/all_to_all | solution.py:253
  23.3 0.6 %pad_maximum_fusion = f32[8,512]{1,0:T(8,128)} fusion(f32[8,128]{1,0:T(8,128)S(1)} %get-tuple-element.22, f32[8,128]{1,0:T(8,128)S(1)} %get-tuple-element.20, f32[8,128]{1,0:T(8,128)S(1)} %get-tuple-element.21, f32[8,128]{1,0:T(8,128)S(1)} %get-tuple-element.19), kind=kLoop, calls=%fused_computation.1 | loop fusion | flops 12288 | bytes 32768 | tf_op jit(solution)/shard_map/concatenate | solution.py:256
  (2 shorter events, 0.0 us)
Async XLA Ops:
  0.0 6.8 %collective-permute-start = (bf16[8,512]{1,0:T(8,128)(2,1)}, bf16[8,512]{1,0:T(8,128)(2,1)S(1)}, u32[]{:S(2)}, u32[]{:S(2)}) collective-permute-start(bf16[8,512]{1,0:T(8,128)(2,1)} %rec_hbm.1), channel_id=1, source_target_pairs={{0,1},{1,0},{2,3},{3,2},{4,5},{5,4},{6,7},{7,6},{8,9},{9,8},{10,11... | collective-permute-start | bytes 24584 | tf_op jit(solution)/shard_map/ppermute | solution.py:208
  1.9 6.0 %collective-permute-start.1 = (bf16[8,512]{1,0:T(8,128)(2,1)}, bf16[8,512]{1,0:T(8,128)(2,1)S(1)}, u32[]{:S(2)}, u32[]{:S(2)}) collective-permute-start(bf16[8,512]{1,0:T(8,128)(2,1)} %rec_hbm.1), channel_id=1, source_target_pairs={{0,8},{1,2},{2,1},{3,4},{4,3},{5,6},{6,5},{7,15},{8,0},{9,10},{10,... | collective-permute-start | bytes 24584 | tf_op jit(solution)/shard_map/ppermute | solution.py:209
